TPU v7x, 32 devices: a whole 2x2x4 slice. The times are simulated.
32 devices in a mesh: rows: 16 (over z, y, x), ch: 2 (over core).
Axes of the slice: x: 2, y: 2, z: 4, core: 2. Of those that a mesh axis runs over, the one named last changes fastest.
Arguments:
- pixels: bfloat16 [32, 917504], P('ch', 'rows'), may hold values from -12 to 12
- skip_map: bfloat16 [64, 229376], P('ch', 'rows'), may hold values from -6 to 6
- style_map: bfloat16 [2048, 28, 256], P('rows'), may hold values from -12 to 12
- crop_rows: int32 [18], replicated, may hold values from 1 to 224, 2048 in all
- crop_group: int32 [18], replicated, may hold values from 0 to 3, as said below
- enc_first: bfloat16 [3, 3, 32, 64], P(None, None, None, 'ch'), may hold values from -0.375 to 0.375
- enc_convs: bfloat16 [3, 3, 3, 64, 64], P(None, None, None, None, 'ch'), may hold values from -0.25 to 0.25
- enc_skip: bfloat16 [32, 64], P(None, 'ch'), may hold values from -1 to 1
- enc_in_gain: float32 [2, 32], P(None, 'ch'), may hold values from 0.1 to 1.9
- enc_in_shift: float32 [2, 32], P(None, 'ch'), may hold values from -2.5 to 2.5
- enc_gain: float32 [3, 64], P(None, 'ch'), may hold values from 0.1 to 1.9
- enc_shift: float32 [3, 64], P(None, 'ch'), may hold values from -2.5 to 2.5
- dec_convs: bfloat16 [4, 3, 3, 64, 64], P(None, None, None, None, 'ch'), may hold values from -0.25 to 0.25
- dec_skip: bfloat16 [64, 64], P(None, 'ch'), may hold values from -0.75 to 0.75
- dec_gain: float32 [5, 64], P(None, 'ch'), may hold values from 0.1 to 1.9
- dec_shift: float32 [5, 64], P(None, 'ch'), may hold values from -2.5 to 2.5
- dense: bfloat16 [3, 256, 64], P(None, None, 'ch'), may hold values from -6 to 6
- out_grad: bfloat16 [64, 229376], P('ch', 'rows'), may hold values from -6 to 6
Outputs:
- decoded: float32 [64, 229376], P('ch', 'rows')
- pixels_grad: float32 [32, 917504], P('ch', 'rows')
- skip_grad: float32 [64, 229376], P('ch', 'rows')
- enc_first_grad: float32 [3, 3, 32, 64], P(None, None, None, 'ch')
- enc_convs_grad: float32 [3, 3, 3, 64, 64], P(None, None, None, None, 'ch')
- enc_skip_grad: float32 [32, 64], P(None, 'ch')
- enc_in_gain_grad: float32 [2, 32], P(None, 'ch')
- enc_in_shift_grad: float32 [2, 32], P(None, 'ch')
- enc_gain_grad: float32 [3, 64], P(None, 'ch')
- enc_shift_grad: float32 [3, 64], P(None, 'ch')
- dec_convs_grad: float32 [4, 3, 3, 64, 64], P(None, None, None, None, 'ch')
- dec_skip_grad: float32 [64, 64], P(None, 'ch')
- dec_gain_grad: float32 [5, 64], P(None, 'ch')
- dec_shift_grad: float32 [5, 64], P(None, 'ch')
- dense_grad: float32 [3, 256, 64], P(None, None, 'ch')
Inputs may be any that keep to these rules, and one draw needn't show every extreme that they name: `crop_rows`: the crops lie one after another from row 0 and fill all 2048 pooled rows; the tallest has exactly 224 rows. `crop_group`: group 0 and group 3 each hold at least one crop; at least one group holds none.
All inputs are finite; a program needn't handle non-finite values.
Results may differ from a plain program's by a relative error of at most 0.025.
Values may be sent and summed in bfloat16 or wider, within the bound.
No kernel may reach another device: no remote copies, remote signals or barrier semaphores. Data moves between devices by JAX's collectives and lax.ppermute only.
A program may use at most 384 MiB of HBM per device.

v0:
```python
import jax
import jax.numpy as jnp
from jax import lax
from jax.sharding import PartitionSpec as P

FULL_W = 224
GROUPS = 4
POOL_W = 112


epsilon = 1e-05
precise = lax.Precision.HIGHEST


def padded_2(cells, sides, width):
    for axis, dim in sides:
        count = lax.axis_size(axis)
        ends = count - 1
        head = lax.slice_in_dim(cells, 0, width, axis=dim)
        tail = lax.slice_in_dim(cells, cells.shape[dim] - width, cells.shape[dim], axis=dim)
        cells = jnp.concatenate(
            [
                lax.ppermute(tail, axis, [(i, (i + 1) % count) for i in range(ends)]),
                cells,
                lax.ppermute(head, axis, [((i + 1) % count, i) for i in range(ends)]),
            ],
            axis=dim,
        )
    return cells


def to_maps(flat, width):
    return jnp.transpose(flat.reshape(flat.shape[0], -1, width), (1, 2, 0))


def from_maps(maps):
    return jnp.transpose(maps, (2, 0, 1)).reshape(maps.shape[2], -1)


def crop_of(row_ids, crop_ends):
    return jnp.sum((row_ids[:, None] >= crop_ends[None, :]).astype(jnp.int32), axis=1)


def patches(extended, up_keep, down_keep, backward):
    strip_rows = extended.shape[0] - 2
    pool_width = extended.shape[1]
    if backward:
        sources = (
            (extended[2:], up_keep[2:]),
            (extended[1:-1], None),
            (extended[:-2], down_keep[:-2]),
        )
    else:
        sources = (
            (extended[:-2], up_keep[1:-1]),
            (extended[1:-1], None),
            (extended[2:], down_keep[1:-1]),
        )
    pieces = []
    for source, keeper in sources:
        if keeper is not None:
            source = source * keeper[:, None, None].astype(source.dtype)
        padded = jnp.pad(source, ((0, 0), (1, 1), (0, 0)))
        for column in range(3):
            offset = 2 - column if backward else column
            pieces.append(padded[:, offset : offset + pool_width])
    return jnp.concatenate(pieces, axis=2).reshape(strip_rows * pool_width, -1)


def conv_input(activation):
    extended = padded_2(activation, (("rows", 0),), 1)
    padded_whole = lax.all_gather(extended, "ch", axis=2, tiled=True)
    return padded_whole


def conv_apply(extended, kernel, up_keep, down_keep):
    strip_rows = extended.shape[0] - 2
    columns = patches(extended, up_keep, down_keep, False)
    result = jnp.dot(
        columns, kernel.reshape(-1, kernel.shape[3]), preferred_element_type=jnp.float32
    )
    return result.reshape(strip_rows, extended.shape[1], kernel.shape[3])


def spread(partial_sum):
    return lax.psum_scatter(partial_sum, "ch", scatter_dimension=2, tiled=True)


def conv_back(gradient, extended, kernel, up_keep, down_keep):
    strip_rows, pool_width, outputs = gradient.shape
    rounded = gradient.astype(jnp.bfloat16)
    grad_ext = padded_2(rounded, (("rows", 0),), 1)
    columns = patches(grad_ext, up_keep, down_keep, True)
    flipped = jnp.transpose(kernel, (0, 1, 3, 2)).reshape(-1, kernel.shape[2])
    partial_sum = jnp.dot(columns, flipped, preferred_element_type=jnp.float32)
    input_grad = spread(partial_sum.reshape(strip_rows, pool_width, kernel.shape[2]))
    forward_cols = patches(extended, up_keep, down_keep, False)
    kernel_grad = lax.dot_general(
        forward_cols,
        rounded.reshape(strip_rows * pool_width, outputs),
        (((0,), (0,)), ((), ())),
        preferred_element_type=jnp.float32,
    )
    return (input_grad, kernel_grad.reshape(kernel.shape))


def skip_apply(normed, kernel):
    whole = lax.all_gather(normed, "ch", axis=2, tiled=True)
    result = jnp.einsum("rwc,cd->rwd", whole, kernel, preferred_element_type=jnp.float32)
    return (whole, result)


def skip_back(gradient, whole, kernel):
    rounded = gradient.astype(jnp.bfloat16)
    partial_sum = jnp.einsum("rwd,cd->rwc", rounded, kernel, preferred_element_type=jnp.float32)
    input_grad = spread(partial_sum)
    kernel_grad = jnp.einsum("rwc,rwd->cd", whole, rounded, preferred_element_type=jnp.float32)
    return (input_grad, kernel_grad)


def moments(values):
    return jnp.stack([jnp.sum(values, axis=(0, 1)), jnp.sum(values * values, axis=(0, 1))])


def settle(totals, pixel_count):
    center = totals[0] / pixel_count
    variance = totals[1] / pixel_count - center * center
    return (center, lax.rsqrt(variance + epsilon))


def statistics(values, pixel_count):
    return settle(lax.psum(moments(values), "rows"), pixel_count)


def norm_act(values, pixel_count, norm_gain, norm_shift):
    center, inv_scale = statistics(values, pixel_count)
    centred = (values - center) * inv_scale
    before = centred * norm_gain + norm_shift
    return (centred, inv_scale, before, conv_input(jax.nn.gelu(before).astype(jnp.bfloat16)))


def gelu_back(before, gradient):
    _, pullback = jax.vjp(jax.nn.gelu, before)
    return pullback(gradient)[0]


def norm_back(gradients, norm_gains, centred, inv_scale, pixel_count):
    pieces = []
    for gradient in gradients:
        pieces.append(jnp.sum(gradient, axis=(0, 1)))
        pieces.append(jnp.sum(gradient * centred, axis=(0, 1)))
    totals = lax.psum(jnp.stack(pieces), "rows")
    result = jnp.zeros_like(centred)
    for position, gradient in enumerate(gradients):
        shift_total = totals[2 * position]
        gain_total = totals[2 * position + 1]
        result = result + norm_gains[position] * inv_scale * (
            gradient - shift_total / pixel_count - centred * gain_total / pixel_count
        )
    return (result, totals)


def per_device(
    pixels,
    skip_map,
    style_map,
    crop_rows,
    crop_group,
    enc_first,
    enc_convs,
    enc_skip,
    enc_in_gain,
    enc_in_shift,
    enc_gain,
    enc_shift,
    dec_convs,
    dec_skip,
    dec_gain,
    dec_shift,
    dense,
    out_grad,
):
    pool_width = POOL_W
    strip_rows = skip_map.shape[1] // pool_width
    pixel_count = lax.axis_size("rows") * strip_rows * pool_width
    first_row = lax.axis_index("rows") * strip_rows
    crop_ends = jnp.cumsum(crop_rows)
    crop_count = crop_rows.shape[0]
    nearby = crop_of(first_row - 2 + jnp.arange(strip_rows + 4, dtype=jnp.int32), crop_ends)
    up_keep = (nearby[1:-1] == nearby[:-2]).astype(jnp.float32)
    down_keep = (nearby[1:-1] == nearby[2:]).astype(jnp.float32)
    member_rows = (
        nearby[2:-2][:, None] == jnp.arange(crop_count, dtype=jnp.int32)[None, :]
    ).astype(jnp.float32)
    full_res = to_maps(pixels, FULL_W).astype(jnp.float32)
    pooled = jnp.mean(
        full_res.reshape(strip_rows, 2, pool_width, 2, full_res.shape[2]), axis=(1, 3)
    )
    style_local = jnp.dot(
        member_rows.T, jnp.sum(style_map.astype(jnp.float32), axis=1), precision=precise
    )
    pooled_center, pooled_scale = statistics(pooled, pixel_count)
    style_totals = lax.psum(style_local, "rows")
    group_member = (crop_group[:, None] == jnp.arange(GROUPS, dtype=jnp.int32)[None, :]).astype(
        jnp.float32
    )
    group_totals = jnp.dot(group_member.T, style_totals, precision=precise)
    group_pixels = jnp.dot(
        group_member.T, crop_rows.astype(jnp.float32) * style_map.shape[1], precision=precise
    )
    group_means = group_totals / jnp.maximum(group_pixels, 1.0)[:, None]
    group_unit = group_means * lax.rsqrt(
        jnp.sum(group_means * group_means, axis=1, keepdims=True) + 1e-06
    )
    crop_style = jnp.dot(group_member, group_unit, precision=precise)
    dense_float = dense.astype(jnp.float32)
    feature_rows = [
        jnp.dot(
            member_rows,
            jnp.dot(crop_style, dense_float[layer], precision=precise),
            precision=precise,
        )[:, None, :]
        for layer in range(3)
    ]
    unit_p = (pooled - pooled_center) * pooled_scale
    before_a0 = unit_p * enc_in_gain[1] + enc_in_shift[1]
    padded_a0 = conv_input(jax.nn.gelu(before_a0).astype(jnp.bfloat16))
    normed_s0 = (unit_p * enc_in_gain[0] + enc_in_shift[0]).astype(jnp.bfloat16)
    hidden_h0 = conv_apply(padded_a0, enc_first, up_keep, down_keep)
    whole_s0, skip_e1 = skip_apply(normed_s0, enc_skip)
    unit_h0, scale_h0, before_h0, padded_a1 = norm_act(
        hidden_h0, pixel_count, enc_gain[0], enc_shift[0]
    )
    section_e1 = skip_e1 + conv_apply(padded_a1, enc_convs[0], up_keep, down_keep)
    unit_e1, scale_e1, before_e1, padded_a2 = norm_act(
        section_e1, pixel_count, enc_gain[1], enc_shift[1]
    )
    hidden_h2 = conv_apply(padded_a2, enc_convs[1], up_keep, down_keep)
    unit_h2, scale_h2, before_h2, padded_a3 = norm_act(
        hidden_h2, pixel_count, enc_gain[2], enc_shift[2]
    )
    section_e2 = section_e1 + conv_apply(padded_a3, enc_convs[2], up_keep, down_keep)
    center_e2, scale_e2 = statistics(section_e2, pixel_count)
    unit_e2 = (section_e2 - center_e2) * scale_e2
    before_b0 = unit_e2 * dec_gain[1] + dec_shift[1]
    padded_b0 = conv_input(jax.nn.gelu(before_b0).astype(jnp.bfloat16))
    normed_q0 = (unit_e2 * dec_gain[0] + dec_shift[0]).astype(jnp.bfloat16)
    skip_field = to_maps(skip_map, pool_width).astype(jnp.float32)
    section_u1 = (
        conv_apply(padded_b0, dec_convs[0], up_keep, down_keep) + skip_field + feature_rows[0]
    )
    unit_u1, scale_u1, before_u1, padded_b1 = norm_act(
        section_u1, pixel_count, dec_gain[2], dec_shift[2]
    )
    whole_q0, skip_d1 = skip_apply(normed_q0, dec_skip)
    section_d1 = skip_d1 + conv_apply(padded_b1, dec_convs[1], up_keep, down_keep)
    section_u2 = section_d1 + skip_field + feature_rows[1]
    unit_u2, scale_u2, before_u2, padded_b2 = norm_act(
        section_u2, pixel_count, dec_gain[3], dec_shift[3]
    )
    section_u3 = conv_apply(padded_b2, dec_convs[2], up_keep, down_keep) + feature_rows[2]
    unit_u3, scale_u3, before_u3, padded_b3 = norm_act(
        section_u3, pixel_count, dec_gain[4], dec_shift[4]
    )
    decoded = section_d1 + conv_apply(padded_b3, dec_convs[3], up_keep, down_keep)
    top_grad = to_maps(out_grad, pool_width).astype(jnp.float32)
    grad_b3, kernel_d3 = conv_back(top_grad, padded_b3, dec_convs[3], up_keep, down_keep)
    grad_u3, norm_u3 = norm_back(
        (gelu_back(before_u3, grad_b3),), dec_gain[4:5], unit_u3, scale_u3, pixel_count
    )
    grad_b2, kernel_d2 = conv_back(grad_u3, padded_b2, dec_convs[2], up_keep, down_keep)
    grad_u2, norm_u2 = norm_back(
        (gelu_back(before_u2, grad_b2),), dec_gain[3:4], unit_u2, scale_u2, pixel_count
    )
    grad_d1 = top_grad + grad_u2
    grad_b1, kernel_d1 = conv_back(grad_d1, padded_b1, dec_convs[1], up_keep, down_keep)
    grad_q0, skip_kernel_d = skip_back(grad_d1, whole_q0, dec_skip)
    grad_u1, norm_u1 = norm_back(
        (gelu_back(before_u1, grad_b1),), dec_gain[2:3], unit_u1, scale_u1, pixel_count
    )
    grad_b0, kernel_d0 = conv_back(grad_u1, padded_b0, dec_convs[0], up_keep, down_keep)
    grad_e2, norm_e2 = norm_back(
        (grad_q0, gelu_back(before_b0, grad_b0)), dec_gain[0:2], unit_e2, scale_e2, pixel_count
    )
    dense_terms = []
    for layer_grad in (grad_u1, grad_u2, grad_u3):
        crop_grad = jnp.dot(member_rows.T, jnp.sum(layer_grad, axis=1), precision=precise)
        dense_terms.append(jnp.dot(crop_style.T, crop_grad, precision=precise))
    grad_a3, kernel_e3 = conv_back(grad_e2, padded_a3, enc_convs[2], up_keep, down_keep)
    grad_h2, norm_h2 = norm_back(
        (gelu_back(before_h2, grad_a3),), enc_gain[2:3], unit_h2, scale_h2, pixel_count
    )
    grad_a2, kernel_e2 = conv_back(grad_h2, padded_a2, enc_convs[1], up_keep, down_keep)
    through_e1, norm_e1 = norm_back(
        (gelu_back(before_e1, grad_a2),), enc_gain[1:2], unit_e1, scale_e1, pixel_count
    )
    grad_e1 = grad_e2 + through_e1
    grad_a1, kernel_e1 = conv_back(grad_e1, padded_a1, enc_convs[0], up_keep, down_keep)
    grad_s0, skip_kernel_e = skip_back(grad_e1, whole_s0, enc_skip)
    grad_h0, norm_h0 = norm_back(
        (gelu_back(before_h0, grad_a1),), enc_gain[0:1], unit_h0, scale_h0, pixel_count
    )
    grad_a0, kernel_first = conv_back(grad_h0, padded_a0, enc_first, up_keep, down_keep)
    grad_p, norm_p = norm_back(
        (grad_s0, gelu_back(before_a0, grad_a0)), enc_in_gain, unit_p, pooled_scale, pixel_count
    )
    channels_in = grad_p.shape[2]
    pixel_maps_grad = jnp.broadcast_to(
        grad_p[:, None, :, None, :] * 0.25, (strip_rows, 2, pool_width, 2, channels_in)
    ).reshape(2 * strip_rows, 2 * pool_width, channels_in)
    skip_maps_grad = grad_u1 + grad_u2
    first_total, enc_total, eskip_total, dec_total, dskip_total, dense_total = lax.psum(
        (
            kernel_first,
            jnp.stack([kernel_e1, kernel_e2, kernel_e3]),
            skip_kernel_e,
            jnp.stack([kernel_d0, kernel_d1, kernel_d2, kernel_d3]),
            skip_kernel_d,
            jnp.stack(dense_terms),
        ),
        "rows",
    )
    enc_in_gain_grad = jnp.stack([norm_p[1], norm_p[3]])
    enc_in_shift_grad = jnp.stack([norm_p[0], norm_p[2]])
    enc_gain_grad = jnp.stack([norm_h0[1], norm_e1[1], norm_h2[1]])
    enc_shift_grad = jnp.stack([norm_h0[0], norm_e1[0], norm_h2[0]])
    dec_gain_grad = jnp.stack([norm_e2[1], norm_e2[3], norm_u1[1], norm_u2[1], norm_u3[1]])
    dec_shift_grad = jnp.stack([norm_e2[0], norm_e2[2], norm_u1[0], norm_u2[0], norm_u3[0]])
    return (
        from_maps(decoded),
        from_maps(pixel_maps_grad),
        from_maps(skip_maps_grad),
        first_total,
        enc_total,
        eskip_total,
        enc_in_gain_grad,
        enc_in_shift_grad,
        enc_gain_grad,
        enc_shift_grad,
        dec_total,
        dskip_total,
        dec_gain_grad,
        dec_shift_grad,
        dense_total,
    )


def solution(mesh):
    placed = (
        P("ch", "rows"),
        P("ch", "rows"),
        P("rows", None, None),
        P(),
        P(),
        P(None, None, None, "ch"),
        P(None, None, None, None, "ch"),
        P(None, "ch"),
        P(None, "ch"),
        P(None, "ch"),
        P(None, "ch"),
        P(None, "ch"),
        P(None, None, None, None, "ch"),
        P(None, "ch"),
        P(None, "ch"),
        P(None, "ch"),
        P(None, None, "ch"),
        P("ch", "rows"),
    )
    return jax.shard_map(
        per_device,
        mesh=mesh,
        in_specs=placed,
        out_specs=(
            P("ch", "rows"),
            P("ch", "rows"),
            P("ch", "rows"),
            P(None, None, None, "ch"),
            P(None, None, None, None, "ch"),
            P(None, "ch"),
            P(None, "ch"),
            P(None, "ch"),
            P(None, "ch"),
            P(None, "ch"),
            P(None, None, None, None, "ch"),
            P(None, "ch"),
            P(None, "ch"),
            P(None, "ch"),
            P(None, None, "ch"),
        ),
        check_vma=False,
    )
```

profile of v0, /device:TPU:0, one launch (start us, length us, event | category | flops | bytes accessed | tf_op | source)
XLA Modules:
  0.0 2128.5 jit_solution(3210339688025271913)
XLA Ops:
  7.2 5.1 reshape.714
  12.4 15.1 copy.194
  27.5 80.4 %reduce_sum.387 = f32[128,112,16]{2,1,0:T(8,128)} reduce(f32[128,2,112,2,16]{4,3,2,1,0:T(2,128)} %bitcast.531, f32[]{:T(128)} %constant.79.clone.1), dimensions={1,3}, to_apply=%region_0.0 | reduce | flops 688128 | bytes 4587524 | tf_op jit(solution)/shard_map/reduce_sum | solution.py:196
  107.9 5.0 copy.195
  113.2 43.7 %psum.161 = f32[2,16]{1,0:T(2,128)S(1)} all-reduce(f32[2,16]{1,0:T(2,128)S(1)} %pad_maximum_fusion.31), channel_id=1, replica_groups=mesh['rows'=16,'ch'=2] {'rows'}, use_global_device_ids=true, to_apply=%region_3.4 | all-reduce | flops 32 | bytes 256 | tf_op jit(solution)/shard_map/psum | solution.py:132
  161.6 10.5 collective-permute-done
  181.3 39.1 %psum.162 = f32[2,32]{1,0:T(2,128)S(1)} all-reduce(f32[2,32]{1,0:T(2,128)S(1)} %pad_maximum_fusion.32), channel_id=1, replica_groups=mesh['rows'=16,'ch'=2] {'rows'}, use_global_device_ids=true, to_apply=%region_8.9 | all-reduce | flops 64 | bytes 512 | tf_op jit(solution)/shard_map/psum | solution.py:132
  263.6 42.0 %psum.163 = f32[2,32]{1,0:T(2,128)S(1)} all-reduce(f32[2,32]{1,0:T(2,128)S(1)} %pad_maximum_fusion.33), channel_id=1, replica_groups=mesh['rows'=16,'ch'=2] {'rows'}, use_global_device_ids=true, to_apply=%region_11.12 | all-reduce | flops 64 | bytes 512 | tf_op jit(solution)/shard_map/psum | solution.py:132
  325.5 9.8 all-gather.11.cloned.1.call-done
  350.2 42.4 %psum.164 = f32[2,32]{1,0:T(2,128)S(1)} all-reduce(f32[2,32]{1,0:T(2,128)S(1)} %pad_maximum_fusion.34), channel_id=1, replica_groups=mesh['rows'=16,'ch'=2] {'rows'}, use_global_device_ids=true, to_apply=%region_14.15 | all-reduce | flops 64 | bytes 512 | tf_op jit(solution)/shard_map/psum | solution.py:132
  417.0 7.2 all-gather.13.cloned.1.call-done
  439.2 77.0 %all-reduce.49 = (f32[2,32]{1,0:T(2,128)S(1)}, f32[18,256]{1,0:T(8,128)S(1)}) all-reduce(f32[2,32]{1,0:T(2,128)S(1)} %pad_maximum_fusion.35, f32[18,256]{1,0:T(8,128)S(1)} %fusion.80), channel_id=1, replica_groups=mesh['rows'=16,'ch'=2] {'rows'}, use_global_device_ids=true, to_apply=%region_17.18 | all-reduce | flops 4672 | bytes 37376 | tf_op jit(solution)/shard_map/psum | solution.py:132
  558.7 42.4 %psum.167 = f32[2,32]{1,0:T(2,128)S(1)} all-reduce(f32[2,32]{1,0:T(2,128)S(1)} %pad_maximum_fusion.36), channel_id=1, replica_groups=mesh['rows'=16,'ch'=2] {'rows'}, use_global_device_ids=true, to_apply=%region_23.24 | all-reduce | flops 64 | bytes 512 | tf_op jit(solution)/shard_map/psum | solution.py:132
  651.7 5.5 fusion.154
  658.7 38.3 %psum.168 = f32[2,32]{1,0:T(2,128)S(1)} all-reduce(f32[2,32]{1,0:T(2,128)S(1)} %pad_maximum_fusion.37), channel_id=1, replica_groups=mesh['rows'=16,'ch'=2] {'rows'}, use_global_device_ids=true, to_apply=%region_26.27 | all-reduce | flops 64 | bytes 512 | tf_op jit(solution)/shard_map/psum | solution.py:132
  723.3 5.5 all-gather.21.cloned.1.call-done
  737.6 4.9 add_reduce_fusion
  745.4 41.9 %psum.169 = f32[2,32]{1,0:T(2,128)S(1)} all-reduce(f32[2,32]{1,0:T(2,128)S(1)} %pad_maximum_fusion.38), channel_id=1, replica_groups=mesh['rows'=16,'ch'=2] {'rows'}, use_global_device_ids=true, to_apply=%region_29.30 | all-reduce | flops 64 | bytes 512 | tf_op jit(solution)/shard_map/psum | solution.py:132
  787.4 5.5 fusion.153
  793.0 36.6 %psum.170 = f32[2,32]{1,0:T(2,128)S(1)} all-reduce(f32[2,32]{1,0:T(2,128)S(1)} %pad_maximum_fusion.39), channel_id=1, replica_groups=mesh['rows'=16,'ch'=2] {'rows'}, use_global_device_ids=true, to_apply=%region_33.34 | all-reduce | flops 64 | bytes 512 | tf_op jit(solution)/shard_map/psum | solution.py:152
  858.7 7.1 fusion.213
  865.9 10.3 reduce-scatter.13.cloned.1.call-done
  876.2 5.1 fusion.152
  881.3 41.9 %psum.171 = f32[2,32]{1,0:T(2,128)S(1)} all-reduce(f32[2,32]{1,0:T(2,128)S(1)} %pad_maximum_fusion.40), channel_id=1, replica_groups=mesh['rows'=16,'ch'=2] {'rows'}, use_global_device_ids=true, to_apply=%region_37.38 | all-reduce | flops 64 | bytes 512 | tf_op jit(solution)/shard_map/psum | solution.py:152
  951.4 7.1 fusion.214
  970.6 42.3 %psum.172 = f32[2,32]{1,0:T(2,128)S(1)} all-reduce(f32[2,32]{1,0:T(2,128)S(1)} %pad_maximum_fusion.41), channel_id=1, replica_groups=mesh['rows'=16,'ch'=2] {'rows'}, use_global_device_ids=true, to_apply=%region_44.45 | all-reduce | flops 64 | bytes 512 | tf_op jit(solution)/shard_map/psum | solution.py:152
  1036.0 9.6 reduce-scatter.19.cloned.1.call-done
  1050.2 42.1 %psum.173 = f32[4,32]{1,0:T(4,128)S(1)} all-reduce(f32[4,32]{1,0:T(4,128)S(1)} %pad_maximum_fusion.27), channel_id=1, replica_groups=mesh['rows'=16,'ch'=2] {'rows'}, use_global_device_ids=true, to_apply=%region_48.49 | all-reduce | flops 128 | bytes 1024 | tf_op jit(solution)/shard_map/psum | solution.py:152
  1120.2 7.1 fusion.216
  1127.6 7.3 reduce-scatter.21.cloned.1.call-done
  1139.4 41.9 %psum.174 = f32[2,32]{1,0:T(2,128)S(1)} all-reduce(f32[2,32]{1,0:T(2,128)S(1)} %pad_maximum_fusion.42), channel_id=1, replica_groups=mesh['rows'=16,'ch'=2] {'rows'}, use_global_device_ids=true, to_apply=%region_52.53 | all-reduce | flops 64 | bytes 512 | tf_op jit(solution)/shard_map/psum | solution.py:152
  1207.0 7.1 fusion.217
  1236.1 37.5 %psum.175 = f32[2,32]{1,0:T(2,128)S(1)} all-reduce(f32[2,32]{1,0:T(2,128)S(1)} %pad_maximum_fusion.43), channel_id=1, replica_groups=mesh['rows'=16,'ch'=2] {'rows'}, use_global_device_ids=true, to_apply=%region_56.57 | all-reduce | flops 64 | bytes 512 | tf_op jit(solution)/shard_map/psum | solution.py:152
  1306.8 7.1 fusion.218
  1320.2 13.1 copy.280
  1333.3 18.7 reshape.686
  1352.0 24.0 %copy.282 = bf16[128,112,576]{1,0,2:T(8,128)(2,1)} copy(bf16[128,112,576]{0,2,1:T(8,128)(2,1)} %copy-done.14) | data formatting | bytes 33030144 | tf_op jit(solution)/shard_map/concatenate | solution.py:67
  1376.0 35.4 %reshape.688 = bf16[14336,576]{0,1:T(8,128)(2,1)} reshape(bf16[128,112,576]{1,0,2:T(8,128)(2,1)} %copy.282) | data formatting | bytes 33030144 | tf_op jit(solution)/shard_map/reshape | solution.py:67
  1411.4 24.0 %copy.284 = bf16[128,112,576]{1,0,2:T(8,128)(2,1)} copy(bf16[128,112,576]{0,2,1:T(8,128)(2,1)} %copy-done.18) | data formatting | bytes 33030144 | tf_op jit(solution)/shard_map/concatenate | solution.py:67
  1435.4 35.4 %reshape.691 = bf16[14336,576]{0,1:T(8,128)(2,1)} reshape(bf16[128,112,576]{1,0,2:T(8,128)(2,1)} %copy.284) | data formatting | bytes 33030144 | tf_op jit(solution)/shard_map/reshape | solution.py:67
  1470.8 24.0 %copy.286 = bf16[128,112,576]{1,0,2:T(8,128)(2,1)} copy(bf16[128,112,576]{0,2,1:T(8,128)(2,1)} %copy-done.15) | data formatting | bytes 33030144 | tf_op jit(solution)/shard_map/concatenate | solution.py:67
  1494.8 35.4 %reshape.694 = bf16[14336,576]{0,1:T(8,128)(2,1)} reshape(bf16[128,112,576]{1,0,2:T(8,128)(2,1)} %copy.286) | data formatting | bytes 33030144 | tf_op jit(solution)/shard_map/reshape | solution.py:67
  1530.2 24.0 %copy.288 = bf16[128,112,576]{1,0,2:T(8,128)(2,1)} copy(bf16[128,112,576]{0,2,1:T(8,128)(2,1)} %copy-done.19) | data formatting | bytes 33030144 | tf_op jit(solution)/shard_map/concatenate | solution.py:67
  1554.2 35.4 %reshape.697 = bf16[14336,576]{0,1:T(8,128)(2,1)} reshape(bf16[128,112,576]{1,0,2:T(8,128)(2,1)} %copy.288) | data formatting | bytes 33030144 | tf_op jit(solution)/shard_map/reshape | solution.py:67
  1589.6 24.0 %copy.290 = bf16[128,112,576]{1,0,2:T(8,128)(2,1)} copy(bf16[128,112,576]{0,2,1:T(8,128)(2,1)} %copy-done.16) | data formatting | bytes 33030144 | tf_op jit(solution)/shard_map/concatenate | solution.py:67
  1613.6 35.4 %reshape.700 = bf16[14336,576]{0,1:T(8,128)(2,1)} reshape(bf16[128,112,576]{1,0,2:T(8,128)(2,1)} %copy.290) | data formatting | bytes 33030144 | tf_op jit(solution)/shard_map/reshape | solution.py:67
  1649.9 24.4 %copy.292 = bf16[128,112,576]{1,0,2:T(8,128)(2,1)} copy(bf16[128,112,576]{0,2,1:T(8,128)(2,1)} %copy-done.17) | data formatting | bytes 33030144 | tf_op jit(solution)/shard_map/concatenate | solution.py:67
  1676.6 35.4 %reshape.703 = bf16[14336,576]{0,1:T(8,128)(2,1)} reshape(bf16[128,112,576]{1,0,2:T(8,128)(2,1)} %copy.292) | data formatting | bytes 33030144 | tf_op jit(solution)/shard_map/reshape | solution.py:67
  1712.5 10.7 convolution_bitcast_fusion.1
  1743.5 23.9 %copy.294 = bf16[128,112,576]{1,0,2:T(8,128)(2,1)} copy(bf16[128,112,576]{0,2,1:T(8,128)(2,1)} %slice_dynamic-update-slice_fusion) | data formatting | bytes 33030144 | tf_op jit(solution)/shard_map/concatenate | solution.py:67
  1767.4 35.6 %reshape.706 = bf16[14336,576]{0,1:T(8,128)(2,1)} reshape(bf16[128,112,576]{1,0,2:T(8,128)(2,1)} %copy.294) | data formatting | bytes 33030144 | tf_op jit(solution)/shard_map/reshape | solution.py:67
  1803.0 9.9 add_bitcast_fusion.1
  1817.9 10.8 convolution_bitcast_fusion
  1835.1 11.0 convolution_bitcast_fusion.2
  1856.5 38.4 %psum.176 = f32[2,32]{1,0:T(2,128)S(1)} all-reduce(f32[2,32]{1,0:T(2,128)S(1)} %pad_maximum_fusion.44), channel_id=1, replica_groups=mesh['rows'=16,'ch'=2] {'rows'}, use_global_device_ids=true, to_apply=%region_63.64 | all-reduce | flops 64 | bytes 512 | tf_op jit(solution)/shard_map/psum | solution.py:152
  1907.9 10.1 convolution_bitcast_fusion.3
  1945.1 9.8 convolution_bitcast_fusion.4
  1959.4 10.7 convolution_bitcast_fusion.5
  1975.3 9.8 convolution_bitcast_fusion.6
  1989.8 5.7 fusion.74
  1999.5 75.5 %all-reduce.48 = (f32[4,16]{1,0:T(4,128)S(1)}, f32[3,3,32,32]{3,2,1,0:T(8,128)}, f32[32,32]{1,0:T(8,128)}, f32[64,32]{0,1:T(8,128)}) all-reduce(f32[4,16]{1,0:T(4,128)S(1)} %pad_maximum_fusion.28, f32[3,3,32,32]{3,2,1,0:T(8,128)S(1)} %fusion.74, ...), channel_id=1, replica_groups=mesh['rows'=16,'ch'=2] {'rows'}, use_global_device_ids=true, to_apply=%region_67.68 | all-reduce | flops 12352 | bytes 98816 | tf_op jit(solution)/shard_map/psum | solution.py:152
  2076.5 5.5 copy.277
  2082.0 17.3 broadcast_in_dim.2
  2099.4 16.8 copy.322
  (827 shorter events, 589.3 us)
Async XLA Ops:
  7.2 630.6 %copy-start = (bf16[64,32]{0,1:T(8,128)(2,1)S(1)}, bf16[64,32]{0,1:T(8,128)(2,1)}, u32[]{:S(2)}) copy-start(bf16[64,32]{0,1:T(8,128)(2,1)} %param.31) | copy-start | bytes 12292
  7.2 240.7 %all-gather.9.cloned.1.call-start = ((), (), s32[]{:S(2)}) async-start(), calls=%async_computation.10 | async-start | bytes 5505024 | tf_op jit(solution)/shard_map/all_gather | solution.py:72
  158.3 13.7 collective-permute-start
  159.7 12.6 collective-permute-start.1
  161.5 144.1 %copy-start.109 = (f32[32]{0:T(128)}, f32[32]{0:T(128)S(1)}, u32[]{:S(2)}) copy-start(f32[32]{0:T(128)S(1)} %get-tuple-element.214) | copy-start | bytes 388
  161.5 144.1 %copy-start.111 = (f32[32]{0:T(128)}, f32[32]{0:T(128)S(1)}, u32[]{:S(2)}) copy-start(f32[32]{0:T(128)S(1)} %get-tuple-element.263) | copy-start | bytes 388
  161.5 231.7 %copy-start.113 = (f32[32]{0:T(128)}, f32[32]{0:T(128)S(1)}, u32[]{:S(2)}) copy-start(f32[32]{0:T(128)S(1)} %get-tuple-element.212) | copy-start | bytes 388
  161.5 231.7 %copy-start.115 = (f32[32]{0:T(128)}, f32[32]{0:T(128)S(1)}, u32[]{:S(2)}) copy-start(f32[32]{0:T(128)S(1)} %get-tuple-element.265) | copy-start | bytes 388
  161.6 567.3 %copy-start.82 = (bf16[128]{0:T(256)(128)(2,1)}, bf16[128]{0:T(256)(128)(2,1)S(1)}, u32[]{:S(2)}) copy-start(bf16[128]{0:T(256)(128)(2,1)S(1)} %get-tuple-element.261) | copy-start | bytes 772
  161.6 571.6 %copy-start.80 = (bf16[128]{0:T(256)(128)(2,1)}, bf16[128]{0:T(256)(128)(2,1)S(1)}, u32[]{:S(2)}) copy-start(bf16[128]{0:T(256)(128)(2,1)S(1)} %get-tuple-element.247) | copy-start | bytes 772
  161.6 1135.2 %copy-start.73 = (bf16[128]{0:T(256)(128)(2,1)}, bf16[128]{0:T(256)(128)(2,1)S(1)}, u32[]{:S(2)}) copy-start(bf16[128]{0:T(256)(128)(2,1)S(1)} %get-tuple-element.262) | copy-start | bytes 772
  161.6 1140.2 %copy-start.78 = (bf16[128]{0:T(256)(128)(2,1)}, bf16[128]{0:T(256)(128)(2,1)S(1)}, u32[]{:S(2)}) copy-start(bf16[128]{0:T(256)(128)(2,1)S(1)} %get-tuple-element.246) | copy-start | bytes 772
  225.2 5.1 collective-permute-start.2
  229.0 5.5 collective-permute-start.3
  238.2 97.1 %all-gather.11.cloned.1.call-start = ((), (), s32[]{:S(2)}) async-start(), calls=%async_computation.11 | async-start | bytes 5505024 | tf_op jit(solution)/shard_map/all_gather | solution.py:72
  239.2 175.6 %copy-start.66 = (bf16[1,3,3,64,32]{3,4,2,1,0:T(8,128)(2,1)}, bf16[1,3,3,64,32]{3,4,2,1,0:T(8,128)(2,1)S(1)}, u32[]{:S(2)}) copy-start(bf16[1,3,3,64,32]{3,4,2,1,0:T(8,128)(2,1)S(1)} %get-tuple-element.176) | copy-start | bytes 110596
  263.5 169.4 %copy-start.20 = (f32[128,112,32]{0,2,1:T(8,128)}, f32[128,112,32]{0,2,1:T(8,128)S(1)}, u32[]{:S(2)}) copy-start(f32[128,112,32]{0,2,1:T(8,128)S(1)} %get-tuple-element.251) | copy-start | bytes 5505028
  310.3 5.1 collective-permute-start.4
  313.8 5.5 collective-permute-start.5
  325.3 98.9 %all-gather.13.cloned.1.call-start = ((), (), s32[]{:S(2)}) async-start(), calls=%async_computation.12 | async-start | bytes 5505024 | tf_op jit(solution)/shard_map/all_gather | solution.py:72
  399.4 4.8 collective-permute-start.6
  403.0 5.5 collective-permute-start.7
  414.4 128.4 %all-gather.17.cloned.1.call-start = ((), (), s32[]{:S(2)}) async-start(), calls=%async_computation.14 | async-start | bytes 5505024 | tf_op jit(solution)/shard_map/all_gather | solution.py:72
  414.7 308.4 %copy-start.148 = (s32[128]{0:T(128)}, s32[128]{0:T(128)S(1)}, u32[]{:S(2)}) copy-start(s32[128]{0:T(128)S(1)} %slice.1063) | copy-start | bytes 1540
  521.6 3.8 collective-permute-start.8
  523.9 5.5 collective-permute-start.9
  533.1 104.7 %all-gather.15.cloned.1.call-start = ((), (), s32[]{:S(2)}) async-start(), calls=%async_computation.13 | async-start | bytes 2752512 | tf_op jit(solution)/shard_map/all_gather | solution.py:108
  538.4 184.6 %copy-start.60 = (f32[18,256]{1,0:T(8,128)}, f32[18,256]{1,0:T(8,128)S(1)}, u32[]{:S(2)}) copy-start(f32[18,256]{1,0:T(8,128)S(1)} %fusion.103) | copy-start | bytes 55300
  538.8 102.2 %all-gather.19.cloned.1.call-start = ((), (), s32[]{:S(2)}) async-start(), calls=%async_computation.15 | async-start | bytes 5505024 | tf_op jit(solution)/shard_map/all_gather | solution.py:72
  605.9 4.8 collective-permute-start.10
  609.4 5.5 collective-permute-start.11
  618.6 110.3 %all-gather.21.cloned.1.call-start = ((), (), s32[]{:S(2)}) async-start(), calls=%async_computation.16 | async-start | bytes 5505024 | tf_op jit(solution)/shard_map/all_gather | solution.py:72
  625.8 7.2 collective-permute-start.16
  628.1 7.1 collective-permute-start.17
  701.7 7.2 collective-permute-start.12
  705.1 6.1 collective-permute-start.13
  717.4 70.0 %reduce-scatter.11.cloned.1.call-start = ((), (), s32[]{:S(2)}) async-start(), calls=%async_computation.18 | async-start | bytes 5505024 | tf_op jit(solution)/shard_map/reduce_scatter | solution.py:86
  722.3 153.9 %reduce-scatter.13.cloned.1.call-start = ((), (), s32[]{:S(2)}) async-start(), calls=%async_computation.19 | async-start | bytes 5505024 | tf_op jit(solution)/shard_map/reduce_scatter | solution.py:86
  836.9 7.0 collective-permute-start.18
  839.3 13.1 collective-permute-start.19
  865.9 100.3 %reduce-scatter.17.cloned.1.call-start = ((), (), s32[]{:S(2)}) async-start(), calls=%async_computation.21 | async-start | bytes 5505024 | tf_op jit(solution)/shard_map/reduce_scatter | solution.py:86
  929.6 7.1 collective-permute-start.20
  932.1 12.9 collective-permute-start.21
  958.5 77.5 %reduce-scatter.15.cloned.1.call-start = ((), (), s32[]{:S(2)}) async-start(), calls=%async_computation.20 | async-start | bytes 5505024 | tf_op jit(solution)/shard_map/reduce_scatter | solution.py:86
  961.6 84.1 %reduce-scatter.19.cloned.1.call-start = ((), (), s32[]{:S(2)}) async-start(), calls=%async_computation.22 | async-start | bytes 5505024 | tf_op jit(solution)/shard_map/reduce_scatter | solution.py:86
  1019.4 6.9 collective-permute-start.22
  1021.7 5.9 collective-permute-start.23
  1036.0 98.9 %reduce-scatter.21.cloned.1.call-start = ((), (), s32[]{:S(2)}) async-start(), calls=%async_computation.23 | async-start | bytes 5505024 | tf_op jit(solution)/shard_map/reduce_scatter | solution.py:86
  1098.6 6.9 collective-permute-start.24
  1100.9 12.9 collective-permute-start.25
  1127.3 104.2 %reduce-scatter.23.cloned.1.call-start = ((), (), s32[]{:S(2)}) async-start(), calls=%async_computation.24 | async-start | bytes 5505024 | tf_op jit(solution)/shard_map/reduce_scatter | solution.py:86
  1185.4 6.9 collective-permute-start.26
  1187.7 12.9 collective-permute-start.27
  1214.2 509.0 %all-gather.23.cloned.1.call-start = ((), (), s32[]{:S(2)}) async-start(), calls=%async_computation.17 | async-start | bytes 5505024 | tf_op jit(solution)/shard_map/all_gather | solution.py:72
  1219.3 5.7 collective-permute-start.14
  1223.7 5.5 collective-permute-start.15
  1280.5 10.8 collective-permute-start.28
  1285.6 566.4 %reduce-scatter.27.cloned.1.call-start = ((), (), s32[]{:S(2)}) async-start(), calls=%async_computation.26 | async-start | bytes 5505024 | tf_op jit(solution)/shard_map/reduce_scatter | solution.py:86
  1286.6 8.0 collective-permute-start.29
  1314.0 682.7 %reduce-scatter.25.cloned.1.call-start = ((), (), s32[]{:S(2)}) async-start(), calls=%async_computation.25 | async-start | bytes 2752512 | tf_op jit(solution)/shard_map/reduce_scatter | solution.py:86
  1851.9 144.8 %reduce-scatter.29.cloned.1.call-start = ((), (), s32[]{:S(2)}) async-start(), calls=%async_computation.27 | async-start | bytes 2752512 | tf_op jit(solution)/shard_map/reduce_scatter | solution.py:86
  1901.0 23.7 %collective-permute-start.30 = (bf16[1,112,32]{1,2,0:T(8,128)(2,1)S(1)}, bf16[1,112,32]{1,2,0:T(8,128)(2,1)S(1)}, u32[]{:S(2)}, u32[]{:S(2)}) collective-permute-start(bf16[1,112,32]{1,2,0:T(8,128)(2,1)S(1)} %copy.272), channel_id=1, source_target_pairs={{2,0},{4,2},{6,4},{8,6},{10,8},{12,10},{14,12},{16,14},{18,16},{20... | collective-permute-start | bytes 21512 | tf_op jit(solution)/shard_map/ppermute | solution.py:25
  1903.3 22.7 %collective-permute-start.31 = (bf16[1,112,32]{1,2,0:T(8,128)(2,1)S(1)}, bf16[1,112,32]{1,2,0:T(8,128)(2,1)S(1)}, u32[]{:S(2)}, u32[]{:S(2)}) collective-permute-start(bf16[1,112,32]{1,2,0:T(8,128)(2,1)S(1)} %copy.274), channel_id=1, source_target_pairs={{0,2},{2,4},{4,6},{6,8},{8,10},{10,12},{12,14},{14,16},{16,18},{18... | collective-permute-start | bytes 21512 | tf_op jit(solution)/shard_map/ppermute | solution.py:23
  1935.6 181.7 %all-reduce.53.cloned.1.call-start = ((), (), s32[]{:S(2)}) async-start(), calls=%async_computation.28 | async-start | bytes 2260992 | tf_op jit(solution)/shard_map/psum | solution.py:312
  (140 other events, 1727.7 us)
Sparse Core Ops, SparseCore 0:
  238.3 9.5 all-gather.8
  325.4 9.8 all-gather.10
  414.5 9.6 all-gather.12
  533.2 9.5 all-gather.16
  544.2 11.3 all-gather.14
  618.7 9.5 all-gather.18
  717.5 11.2 all-gather.20
  731.7 12.7 reduce-scatter.10
  866.0 10.2 reduce-scatter.12
  958.7 7.4 reduce-scatter.16
  969.0 12.6 reduce-scatter.14
  1036.1 9.5 reduce-scatter.18
  1127.5 7.4 reduce-scatter.20
  1214.3 7.4 reduce-scatter.22
  1285.7 11.7 all-gather.22
  1314.1 9.2 reduce-scatter.26
  1852.0 6.9 reduce-scatter.24
  1935.8 6.2 reduce-scatter.28
  1986.5 110.7 all-reduce.52
where the time goes:
time: 2150 us; the launch traced here: 2130 us
  local copies, waits for them, and re-layouts  796 us (37%)
  blocking collectives  729 us (34%)
  other arithmetic  251 us (12%)
  matrix products  177 us (8%)
  waiting for transfers between devices  86.3 us (4%)
  starting transfers between devices  72.5 us (3%)
    psum x8, blocking collectives, statistics(): return settle(lax.psum(moments(values), 'rows'), pixel_count)  367 us
    psum x8, blocking collectives, norm_back(): totals = lax.psum(jnp.stack(pieces), 'rows')  356 us
    reshape x8, local copies, waits for them, and re-layouts, patches(): return jnp.concatenate(pieces, axis=2).reshape(strip_rows * pool_width, -1)  267 us
    concatenate x24, local copies, waits for them, and re-layouts, patches(): return jnp.concatenate(pieces, axis=2).reshape(strip_rows * pool_width, -1)  191 us
    unnamed x415, local copies, waits for them, and re-layouts  104 us
    reduce_sum x1, other arithmetic, per_device(): jnp.mean(full_res.reshape(strip_rows, 2, pool_width, 2, full_res.shape[2]...  80.4 us
    dot_general x8, matrix products, conv_back(): lax.dot_general(forward_cols, rounded.reshape(strip_rows * pool_width, ou...  78.5 us
    ppermute x16, starting transfers between devices, padded_2(): lax.ppermute(tail, axis, [(i, (i + 1) % count) for i in range(ends)])  49.3 us
  transfers between devices with their start and end apart: 51, of which 17 were waited for; matrix products, arithmetic and copies ran while one was open for 41% of the time, Pallas kernels for 0%

commit v1 on v0

v1 whole, which is shorter than its diff:
```python
import functools

import jax
import jax.numpy as jnp
from jax import lax
from jax.experimental import pallas as pl
from jax.experimental.pallas import tpu as pltpu
from jax.sharding import PartitionSpec as P

FULL_W = 224
GROUPS = 4
POOL_W = 112
LANES = 128
HALO = 14
STEP_AHEAD = 32
STEP_BACK = 24

epsilon = 1e-05
gelu_scale = 0.7978845608
gelu_cubic = 0.7978845608 * 0.044715

both = ("rows", "ch")
f32 = jnp.float32
bf16 = jnp.bfloat16

VMEM = pl.BlockSpec(memory_space=pltpu.VMEM)
SMEM = pl.BlockSpec(memory_space=pltpu.SMEM)


def call(kernel, name, ins, outs, scratch=(), limit=5, cost=4, after=()):
    count = len(ins)

    def body(*refs):
        kernel(*refs[:count], *refs[count + len(after) :])

    spaces = {True: SMEM, False: VMEM, "hbm": pl.BlockSpec(memory_space=pltpu.HBM)}
    in_specs = [spaces[kind] for _, kind in ins]
    in_specs += [pl.BlockSpec(memory_space=pl.ANY)] * len(after)
    return pl.pallas_call(
        body,
        name=name,
        out_shape=tuple(jax.ShapeDtypeStruct(out[0], out[1]) for out in outs),
        in_specs=in_specs,
        out_specs=tuple(spaces[out[2] if len(out) > 2 else False] for out in outs),
        scratch_shapes=list(scratch),
        compiler_params=pltpu.CompilerParams(vmem_limit_bytes=limit * 2**20),
        cost_estimate=pl.CostEstimate(
            flops=0, bytes_accessed=int(cost * 3_500_000), transcendentals=0
        ),
    )(*[value for value, _ in ins], *after)


def lanes_of(shape):
    return lax.broadcasted_iota(jnp.int32, shape, len(shape) - 1)


def roll(tile, amount):
    return pltpu.roll(tile, amount % LANES, axis=1)


def dot(lhs, rhs):
    return jnp.dot(lhs, rhs, preferred_element_type=f32)


def gelu(half):
    inner = jnp.tanh(half * (2.0 * gelu_scale + (8.0 * gelu_cubic) * (half * half)))
    return half + half * inner


def gelu_slope(half):
    square = half * half
    inner = jnp.tanh(half * (2.0 * gelu_scale + (8.0 * gelu_cubic) * square))
    slope = gelu_scale + (12.0 * gelu_cubic) * square
    return (0.5 + 0.5 * inner) + (half * slope) * (1.0 - inner * inner)


def total_of(stats, slot, period=1):
    total = None
    for part in stats:
        values = part[:, :LANES]
        if period > 1:
            rows = lax.broadcasted_iota(jnp.int32, values.shape, 0)
            values = jnp.where(rows % period == slot, values, 0.0)
        values = jnp.sum(values, axis=0, keepdims=True)
        total = values if total is None else total + values
    return total


def take(refs, count):
    return [refs.pop(0) for _ in range(count)]


def columns_of(stats, slot, period=1):
    total = total_of(stats, slot, period)
    return jnp.transpose(jnp.broadcast_to(total, (LANES, LANES)))


def row_of(*parts):
    tall = jnp.concatenate(parts, axis=0)
    return jnp.sum(jnp.transpose(tall), axis=0, keepdims=True)


def settle(stats, channels, inv_count):
    columns = columns_of(stats, 0)
    center = columns[:channels] * inv_count
    variance = columns[channels : 2 * channels] * inv_count - center * center
    return center, lax.rsqrt(variance + epsilon)


def affine(center, scale, norm):
    gain = scale * norm[0]
    return gain, norm[1] - center * gain


def halved(columns):
    return [0.5 * value for value in columns]


def inner_only(*columns):
    return [jnp.where(lanes_of(value.shape) < POOL_W, value, 0.0) for value in columns]


def back_columns(sums, slot, channels, first, center, scale, gain, inv_count, period=1):
    columns = columns_of(sums, slot, period)
    shift_sum = columns[first : first + channels] * inv_count
    gain_sum = columns[first + channels : first + 2 * channels] * inv_count
    outer = gain * scale
    slope = outer * scale * gain_sum
    return outer, slope, center * slope - outer * shift_sum


def three_wide(tile):
    low = tile.astype(bf16)
    return [roll(low, 1), low, roll(low, -1)]


def conv_rows(first, count, weights, width, keep, held, produce, emit, extra=None, weigh=None):
    held[...] = jnp.zeros_like(held)

    def chunk(row, height):
        products = []
        sources = []
        for pair in range(height // 2):
            source = jnp.concatenate(
                [jnp.concatenate(produce(row + 2 * pair + k), axis=0) for k in range(2)], axis=1
            )
            products.append(dot(weights(), source))
            sources.append(source)
        if weigh is not None:
            for start in range(0, height, 16):
                size = min(16, height - start)
                weigh(row + start, size, sources[start // 2 : (start + size) // 2])

        def block(group, k):
            lanes = slice(LANES * (k % 2), LANES * (k % 2 + 1))
            return products[k // 2][group * width : (group + 1) * width, lanes]

        links = [keep[0, row + k].astype(f32) for k in range(height)]
        rows = [held[1] + links[0] * block(2, 0)]
        for k in range(height - 1):
            above = held[0] if k == 0 else block(0, k - 1)
            rows.append(links[k] * above + block(1, k) + links[k + 1] * block(2, k + 1))
        last = block(1, height - 1) + links[height - 1] * block(0, height - 2)
        held[0] = block(0, height - 1)
        held[1] = last
        if extra is not None:
            for k in range(height):
                lanes = slice(LANES * (k % 2), LANES * (k % 2 + 1))
                extra(row + k, products[k // 2][3 * width :, lanes])
        emit(row - 1, rows)

    height = STEP_AHEAD if weigh is None else STEP_BACK

    def body(step, carry):
        chunk(first + height * step, height)
        return carry

    steps = count // height
    lax.fori_loop(0, steps, body, 0)
    if count % height:
        chunk(first + height * steps, count % height)


def own_place(row, own_rows):
    return jnp.clip(row - HALO, -2, own_rows + 1) + 2


def own_limit(row, own_rows):
    inside = jnp.logical_and(row >= HALO, row < HALO + own_rows)
    return jnp.where(inside, POOL_W, 0)


def add_stats(acc, row, first_values, second_values, own_rows):
    lanes = lanes_of(first_values[0].shape)
    one = None
    two = None
    for k, (left, right) in enumerate(zip(first_values, second_values)):
        kept = jnp.where(lanes < own_limit(row + k, own_rows), left, 0.0)
        other = kept * right
        one = kept if one is None else one + kept
        two = other if two is None else two + other
    acc[0] += one
    acc[1] += two


def forward_kernel(
    spec, own_rows, inv_count, *refs
):
    (f, cin, cout, has_skip_in, side_norm, features, keep_raw, layer, spots, seen) = spec
    refs = list(refs)
    keep = refs.pop(0)
    values = refs.pop(0)
    stats = take(refs, seen)
    norms = refs.pop(0)
    norm, side = norms.at[spots[0]], norms.at[spots[-1]]
    weight_stack = refs.pop(0)
    depth = 3 * cin + (0 if not has_skip_in else 32 if layer == 1 else 64)

    def weights():
        return weight_stack[layer, :, :depth]

    skip_in = refs.pop(0) if has_skip_in else None
    residual = refs.pop(0) if "residual" in features else None
    skip_map = refs.pop(0) if "skip" in features else None
    feature = refs.pop(0) if "feature" in features else None
    payload = refs.pop(0) if "payload" in features else None
    result = refs.pop(0)
    raw = refs.pop(0) if keep_raw else None
    act = refs.pop(0)
    side_out = refs.pop(0) if side_norm else None
    columns_out = refs.pop(0)
    stats_out = refs.pop(0)
    held = refs.pop(0)
    acc = refs.pop(0)
    acc[...] = jnp.zeros_like(acc)
    center, scale = settle(stats, cin, inv_count)
    columns_out[0] = center
    columns_out[1] = scale
    gain, shift = inner_only(*halved(affine(center, scale, norm)))
    if side_norm:
        side_gain, side_shift = inner_only(*affine(center, scale, side))

    def produce(row):
        value = values[row]
        active = gelu(value * gain + shift)
        pieces = three_wide(active)
        act[own_place(row, own_rows)] = pieces[1]
        if side_norm:
            side_out[row] = (value * side_gain + side_shift).astype(bf16)
        if has_skip_in:
            pieces.append(skip_in[row])
        return pieces

    def emit(row, rows):
        if residual is not None:
            rows = [value + residual[row + k] for k, value in enumerate(rows)]
        if raw is not None:
            for k, value in enumerate(rows):
                raw[own_place(row + k, own_rows)] = value
        if skip_map is not None:
            rows = [value + skip_map[row + k].astype(f32) for k, value in enumerate(rows)]
        if feature is not None:
            turned = pltpu.roll(feature[...], LANES - jnp.maximum(row, 0), axis=1)
            rows = [
                value + jnp.broadcast_to(turned[:, k : k + 1], (cout, LANES))
                for k, value in enumerate(rows)
            ]
        for k, value in enumerate(rows):
            result[jnp.maximum(row + k, 0)] = value
        add_stats(acc, row, rows, rows, own_rows)

    conv_rows(
        HALO - f - 1, own_rows + 2 * f + 2, weights, cout, keep, held, produce, emit
    )
    total = row_of(acc[0], acc[1])
    if payload is not None:
        total = jnp.concatenate([total, payload[...]], axis=1)
    stats_out[...] = jnp.broadcast_to(total, stats_out.shape)


def forward(name, keep, values, stats, norms, spots, weights, layer, f, own_rows, inv_count,
            out_rows, skip_in=None, residual=None, skip_map=None, feature=None, payload=None,
            keep_raw=False, after=()):
    total = own_rows + 2 * HALO
    cin = values.shape[1]
    cout = 64
    features = ()
    outs = []
    side = len(spots) > 1
    ins = [(keep, True), (values, False)]
    ins += [(part, False) for part in stats]
    ins += [(norms, False), (weights, False)]
    if skip_in is not None:
        ins.append((skip_in, False))
    if residual is not None:
        ins.append((residual, False))
        features += ("residual",)
    if skip_map is not None:
        ins.append((skip_map, False))
        features += ("skip",)
    if feature is not None:
        ins.append((feature, False))
        features += ("feature",)
    wide = LANES
    if payload is not None:
        ins.append((payload, False))
        features += ("payload",)
        wide += payload.shape[1]
    outs.append(((total, cout, LANES), f32))
    if keep_raw:
        outs.append(((own_rows + 4, cout, LANES), f32))
    outs.append(((own_rows + 4, cin, LANES), bf16))
    if side:
        outs.append(((total, cin, LANES), bf16))
    outs.append(((2, cin, LANES), f32))
    outs.append(((out_rows, wide), f32))
    spec = (f, cin, cout, skip_in is not None, side, features, keep_raw, layer, spots, len(stats))
    scratch = [pltpu.VMEM((2, cout, LANES), f32), pltpu.VMEM((2, cout, LANES), f32)]
    return call(
        functools.partial(forward_kernel, spec, own_rows, inv_count), name, ins, outs, scratch,
        after=after,
    )


def spread_lines(lines, period, out):
    rows = lax.broadcasted_iota(jnp.int32, out.shape, 0) % period
    value = jnp.zeros(out.shape, f32)
    for k, line in enumerate(lines):
        value = jnp.where(rows == k, jnp.broadcast_to(line, out.shape), value)
    out[...] = value


def group_lines(top, u3, d1, u1):
    lines = []
    for sums in (u1[...], d1[...] - top[...], u3[...]):
        for pair in range(GROUPS // 2):
            left = pltpu.roll(sums[2 * pair : 2 * pair + 1], 64, axis=1)
            right = sums[2 * pair + 1 : 2 * pair + 2]
            lines.append(jnp.where(lanes_of((1, LANES)) < 64, left, right))
    return lines


def decode_kernel(own_rows, keep, core, act, weight_stack, raw, kept, sent, held):
    first = core[0] == 0

    def weights():
        return weight_stack[7, :, :192]

    def produce(row):
        return three_wide(act[own_place(row, own_rows)])

    def emit(row, rows):
        for k, value in enumerate(rows):
            place = own_place(row + k, own_rows)
            value = (value + raw[place]).astype(bf16)
            low, high = value[:32], value[32:]
            kept[place] = jnp.where(first, low, high)
            sent[place] = jnp.where(first, high, low)

    conv_rows(HALO - 1, own_rows + 2, weights, 64, keep, held, produce, emit)


def backward_kernel(spec, own_rows, inv_count, *refs):
    (b, cout, cin, slopes_in, extra_in, below_sides, extra_rows, save, split, skip_rows, export,
     gathers, layer, spots, below_spot, seen) = spec
    refs = list(refs)
    keep = refs.pop(0)
    core = refs.pop(0)
    slopes = [refs.pop(0) for _ in range(slopes_in)]
    if slopes_in:
        values = refs.pop(0)
        columns = refs.pop(0)
        sums = take(refs, seen)
        norm_stack = refs.pop(0)
    norms = [norm_stack.at[spot] for spot in spots]
    extra = refs.pop(0) if extra_in else None
    weight_stack = refs.pop(0)

    def weights():
        return weight_stack[layer, : 3 * cin + extra_rows, :]

    below = refs.pop(0)
    below_columns = refs.pop(0)
    below_norm = refs.pop(0).at[below_spot]
    below_side = refs.pop(0) if below_sides else None
    other = refs.pop(0) if split else None
    act = refs.pop(0) if slopes_in else None
    skip_in = refs.pop(0) if skip_rows else None
    gathered = [refs.pop(0) for _ in range(gathers)]
    pure_out = refs.pop(0) if save else None
    slope_out = refs.pop(0)
    skip_out = refs.pop(0) if extra_rows else None
    kept = refs.pop(0) if split else None
    sent = refs.pop(0) if split else None
    stats_out = refs.pop(0)
    weights_kept = refs.pop(0)
    weights_sent = refs.pop(0)
    groups_out = refs.pop(0) if export else None
    if not slopes_in:
        act = refs.pop(0)
        columns_out = refs.pop(0)
        columns_out[0], columns_out[1] = settle([below_columns], cin, inv_count)
        below_columns = columns_out
    held = refs.pop(0)
    acc = refs.pop(0)
    total = refs.pop(0)
    acc[...] = jnp.zeros_like(acc)
    total[...] = jnp.zeros_like(total)
    first = core[0] == 0
    outers = []
    slope_col = None
    const_col = None
    if slopes_in:
        center, scale = columns[0], columns[1]
    for k, norm in enumerate(norms):
        outer, slope, const = back_columns(
            sums, k, cout, 0, center, scale, norm[0], inv_count, slopes_in
        )
        outers.append(outer)
        slope_col = slope if slope_col is None else slope_col + slope
        const_col = const if const_col is None else const_col + const
    gain, shift = halved(affine(below_columns[0], below_columns[1], below_norm))
    if slopes_in:
        slope_col, const_col, *outers = inner_only(slope_col, const_col, *outers)
    member_rows = lax.broadcasted_iota(jnp.int32, (16, LANES), 0)
    height = 3 * cin + skip_rows + (16 if export else 0)
    if not slopes_in:
        inner_gain, inner_shift = inner_only(gain, shift)

        def active(step, carry):
            for k in range(6):
                row = HALO - 1 + 6 * step + k
                act[6 * step + k + 1] = gelu(below[row] * inner_gain + inner_shift).astype(bf16)
            return carry

        lax.fori_loop(0, (own_rows + 2) // 6, active, 0)
        for row in range((own_rows + 2) // 6 * 6, own_rows + 2):
            act[row + 1] = gelu(below[HALO - 1 + row] * inner_gain + inner_shift).astype(bf16)

    def produce(row):
        if not slopes_in:
            return three_wide(extra[row])
        grad = const_col - values[row] * slope_col
        for slope, outer in zip(slopes, outers):
            grad = grad + slope[row] * outer
        place = own_place(row, own_rows)
        if save:
            pure_out[place if save == "own" else row] = grad
        if split:
            both_grads = grad + other[place]
            both_grads = both_grads.astype(bf16)
            low, high = both_grads[:32], both_grads[32:]
            kept[place] = jnp.where(first, low, high)
            sent[place] = jnp.where(first, high, low)
        if extra is not None:
            grad = grad + extra[row].astype(f32)
        return three_wide(grad)

    def emit(row, rows):
        results = []
        centred = []
        for k, value in enumerate(rows):
            lower = below[row + k]
            half = lower * gain + shift
            slope = gelu_slope(half) * value
            slope_out[own_place(row + k, own_rows) if cin == 32 else row + k] = slope
            results.append(slope)
            centred.append(half)
        add_stats(acc, row, results, centred, own_rows)
        if below_side is not None:
            sides = [
                below_side[own_place(row + k, own_rows) if cin == 32 else row + k]
                for k in range(len(rows))
            ]
            add_stats(acc.at[2:4], row, sides, centred, own_rows)

    def extra_emit(row, value):
        skip_out[own_place(row, own_rows) if extra_rows == 32 else row] = value

    def weigh(row, count, sources):
        lefts = []
        empty = jnp.zeros((cin, LANES), bf16)
        for k in range(count):
            at = row + k
            inside = jnp.logical_and(at >= HALO, at < HALO + own_rows)
            up = jnp.logical_and(inside, keep[0, at] > 0)
            down = jnp.logical_and(inside, keep[0, at + 1] > 0)
            place = jnp.clip(at - HALO, 0, own_rows - 1)
            left = [
                jnp.where(up, act[place + 1], empty),
                jnp.where(inside, act[place + 2], empty),
                jnp.where(down, act[place + 3], empty),
            ]
            if skip_rows:
                left.append(
                    jnp.where(inside, skip_in[at], jnp.zeros((skip_rows, LANES), bf16))
                )
            if export:
                group = jnp.where(inside, keep[1, at], -1)
                left.append((member_rows == group).astype(f32).astype(bf16))
            lefts.append(jnp.concatenate(left, axis=0))
        total[:height, :192] += lax.dot_general(
            jnp.concatenate(lefts, axis=1),
            jnp.concatenate(sources, axis=1),
            NT,
            preferred_element_type=f32,
        )

    conv_rows(
        HALO - b, own_rows + 2 * b, weights, cin, keep, held, produce, emit,
        extra_emit if extra_rows else None, weigh,
    )
    per_gain = 1.0 / below_norm[0]

    def by_unit(plain, halves):
        return (2.0 * halves - below_norm[1] * plain) * per_gain

    one = [acc[0], by_unit(acc[0], acc[1])]
    if below_side is not None:
        two = [acc[2], by_unit(acc[2], acc[3])]
        if cin == 32:
            spread_lines([row_of(*two, *one)] + group_lines(*gathered), 8, stats_out)
        else:
            spread_lines([row_of(*two), row_of(*one)], 2, stats_out)
    else:
        stats_out[...] = jnp.broadcast_to(row_of(*one), stats_out.shape)
    if export:
        groups_out[...] = total[3 * cin + skip_rows : 3 * cin + skip_rows + 8, :LANES]
    for start in range(0, weights_kept.shape[1], LANES):
        tall = total[start : start + LANES]
        turned = [jnp.transpose(tall[:, :LANES]), jnp.transpose(tall[:, LANES:])]
        taps = [turned[1][:64], turned[0][64:], turned[0][:64]]
        low = jnp.concatenate([tap[:32] for tap in taps], axis=0)
        high = jnp.concatenate([tap[32:] for tap in taps], axis=0)
        weights_kept[:, start : start + LANES] = jnp.where(first, low, high)
        weights_sent[:, start : start + LANES] = jnp.where(first, high, low)


def backward(name, keep, core, slopes, values, stats, sums, norms, spots, weights, layer, below,
             below_stats, below_norms, below_spot, act, b, own_rows, inv_count, out_rows,
             extra=None, below_side=None, extra_rows=0, save=False, other=None, skip_in=None,
             after=(), export=False, gathered=()):
    total = own_rows + 2 * HALO
    cout = 64
    cin = below.shape[1]
    ins = [(keep, True), (core, True)]
    split = other is not None
    ins += [(slope, False) for slope in slopes]
    if slopes:
        ins.append((values, False))
        ins.append((stats, False))
        ins += [(part, False) for part in sums]
        ins.append((norms, False))
    if extra is not None:
        ins.append((extra, False))
    ins += [(weights, False), (below, False)]
    ins += [(below_stats, False), (below_norms, False)]
    if below_side is not None:
        ins.append((below_side, False))
    if split:
        ins.append((other, False))
    if slopes:
        ins.append((act, False))
    if skip_in is not None:
        ins.append((skip_in, False))
    ins += [(value, False) for value in gathered]
    outs = []
    if save:
        outs.append(((own_rows + 4 if save == "own" else total, cout, LANES), f32))
    outs.append(((own_rows + 4 if cin == 32 else total, cin, LANES), f32))
    if extra_rows:
        outs.append(((own_rows + 4 if extra_rows == 32 else total, extra_rows, LANES), f32))
    if split:
        outs.append(((own_rows + 4, 32, LANES), bf16))
        outs.append(((own_rows + 4, 32, LANES), bf16))
    tall = out_rows if below_side is None else 2 * out_rows if cin == 64 else 8
    outs.append(((tall, LANES), f32))
    skip_rows = 0 if skip_in is None else skip_in.shape[1]
    height = -(-(3 * cin + skip_rows + 16) // LANES) * LANES
    width = -(-(3 * cin + skip_rows) // LANES) * LANES
    outs += [((96, width), f32), ((96, width), f32)]
    if export:
        outs.append(((8, LANES), f32))
    if not slopes:
        outs.append(((own_rows + 4, cin, LANES), bf16))
        outs.append(((2, cin, LANES), f32))
    spec = (b, cout, cin, len(slopes), extra is not None, below_side is not None, extra_rows,
            save, split, skip_rows, export, len(gathered), layer, spots, below_spot,
            len(sums))
    scratch = [
        pltpu.VMEM((2, cin, LANES), f32), pltpu.VMEM((4, cin, LANES), f32),
        pltpu.VMEM((height, 256), f32),
    ]
    return call(
        functools.partial(backward_kernel, spec, own_rows, inv_count), name, ins, outs, scratch,
        after=after,
    )


SKIP_HALO = 9
TOP_HALO = 8


def entry_kernel(own_rows, core, skip_in, top_in, pixels_in, mine, send_pair, send_same,
                 send_cross, stats_out, acc, skip, top, pixels, pool, maps, pooled_maps, arrived,
                 left):
    strip = 2 * own_rows
    pair_rows = own_rows + HALO
    first = core[0] == 0
    loads = [
        pltpu.make_async_copy(source, target, arrived.at[k])
        for k, (source, target) in enumerate(
            ((skip_in, skip), (top_in, top), (pixels_in, pixels))
        )
    ]
    for load in loads:
        load.start()
    home = pixel_home(lax.broadcasted_iota(jnp.int32, pool.shape, 0))
    pool[...] = jnp.where(home == lanes_of(pool.shape), 0.25, 0.0).astype(bf16)
    acc[...] = jnp.zeros_like(acc)
    wide = 4 * FULL_W
    other = 1 - core[0]
    stores = []

    def send(source, target):
        stores.append(pltpu.make_async_copy(source, target, left.at[len(stores)]))
        stores[-1].start()

    def send_part(local, channels, halos):
        for side, out in ((core[0], mine), (other, send_pair)):
            rows = pl.ds(side * (strip - pair_rows), pair_rows)
            send(local.at[rows], out.at[:, channels])
        for channel, count, at in halos:
            for side, out in ((other, send_same), (core[0], send_cross)):
                rows = pl.ds(side * (strip - count), count)
                send(local.at[rows, channel : channel + 32], out.at[at : at + count])

    loads[0].wait()
    loads[1].wait()
    lanes = lanes_of((32, LANES)).astype(f32).astype(bf16)
    zero = jnp.zeros((32, LANES), bf16)

    def body(step, carry):
        start = pl.multiple_of(step * 8 * POOL_W, LANES)
        for place, source in enumerate((skip, top)):
            flat = source[:, pl.ds(start, 8 * POOL_W)]
            tiles = [flat[:, LANES * k : LANES * (k + 1)] for k in range(7)]
            for k in range(8):
                if k == 0:
                    line = tiles[0]
                elif k == 7:
                    line = roll(tiles[6], 16 * 7)
                else:
                    line = jnp.where(
                        lanes < 16 * k, roll(tiles[k - 1], 16 * k), roll(tiles[k], 16 * k)
                    )
                line = jnp.where(lanes < POOL_W, line, zero)
                maps[8 * step + k, 32 * place : 32 * (place + 1)] = line
        return carry

    lax.fori_loop(0, strip // 8, body, 0)
    send_part(maps, slice(0, 64), ((0, SKIP_HALO, 0), (32, TOP_HALO, SKIP_HALO)))
    loads[2].wait()

    def pool_body(step, carry):
        source = jnp.concatenate(
            [
                pixels[:, pl.ds(pl.multiple_of((8 * step + k) * wide, LANES), wide)]
                for k in range(8)
            ],
            axis=0,
        )
        pooled = dot(source, pool[...])
        one = jnp.zeros((16, LANES), f32)
        two = jnp.zeros((16, LANES), f32)
        for k in range(8):
            for side in range(2):
                value = pooled[16 * k : 16 * (k + 1), LANES * side : LANES * (side + 1)]
                row = 16 * step + 2 * k + side
                upper = value.astype(bf16)
                pooled_maps[row, :16] = upper
                pooled_maps[row, 16:] = (value - upper.astype(f32)).astype(bf16)
                one = one + value
                two = two + value * value
        acc[0] += one
        acc[1] += two
        return carry

    lax.fori_loop(0, strip // 16, pool_body, 0)
    send_part(pooled_maps, slice(64, 96), ((0, HALO, SKIP_HALO + TOP_HALO),))
    empty = jnp.zeros((16, LANES), f32)
    one = acc[0]
    two = acc[1]
    stats = row_of(
        jnp.where(first, one, empty), jnp.where(first, empty, one),
        jnp.where(first, two, empty), jnp.where(first, empty, two),
        jnp.zeros((64, LANES), f32),
    )
    stats_out[...] = jnp.broadcast_to(stats, stats_out.shape)
    for store in stores:
        store.wait()


def crop_kernel(own_rows, strip_rows, style_columns, place, crop_rows, crop_group, meta, members,
                counts):
    crops = crop_rows.shape[0]
    rows = lanes_of((8, LANES)) + place[0] - HALO
    which = lax.broadcasted_iota(jnp.int32, (8, LANES), 0)
    start = jnp.int32(0)
    joined = jnp.zeros((8, LANES), jnp.int32)
    groups = jnp.full((8, LANES), -1, jnp.int32)
    pixels = jnp.zeros((8, LANES), jnp.int32)
    for k in range(crops):
        size = crop_rows[k]
        inside = jnp.logical_and(rows >= start, rows < start + size)
        linked = jnp.logical_and(rows > start, rows < start + size)
        joined = jnp.where(linked, 1, joined)
        groups = jnp.where(inside, crop_group[k], groups)
        pixels = pixels + jnp.where(which == crop_group[k], size * style_columns, 0)
        start = start + size
    meta[...] = jnp.where(which == 0, joined, groups)
    members[...] = (groups == which).astype(f32)
    counts[...] = jnp.maximum(pixels, 1).astype(f32)


def pack_kernel(enc_first, enc, dec, eskip, dskip, dense, in_gain, in_shift, enc_gain,
                enc_shift, dec_gain, dec_shift, out, small):
    taps = [enc[k, i, j] for k in range(3) for i in range(3) for j in range(3)]
    taps += [dec[k, i, j] for k in range(4) for i in range(3) for j in range(3)]
    taps.append(dskip[...])
    for k in range(32):
        pair = [tap.astype(f32) for tap in taps[2 * k : 2 * k + 2]]
        out[k] = jnp.concatenate(pair, axis=1).astype(bf16)
    quarters = [enc_first[i, j].astype(f32) for i in range(3) for j in range(3)]
    quarters.append(eskip[...].astype(f32))
    quarters += [jnp.zeros((32, 32), f32)] * 2
    for k in range(3):
        out[32 + k] = jnp.concatenate(quarters[4 * k : 4 * k + 4], axis=1).astype(bf16)
    for k in range(6):
        out[35 + k] = dense[k // 2, :, LANES * (k % 2) : LANES * (k % 2 + 1)]
    small[...] = jnp.zeros_like(small)
    at = 0
    for source in (in_gain, in_shift, enc_gain, enc_shift, dec_gain, dec_shift):
        count, width = source.shape
        small[at : at + count, :width] = source[...]
        at += count
    rest = small[...]
    for k in range(3):
        part = rest.astype(bf16)
        out[41 + k] = part
        rest = rest - part.astype(f32)


def style_sum_kernel(own_rows, core, style, members, out):
    start = pl.multiple_of(core[0] * own_rows, own_rows)
    total = style[0, pl.ds(start, own_rows), :].astype(f32)
    for column in range(1, style.shape[0]):
        total = total + style[column, pl.ds(start, own_rows), :].astype(f32)
    here = pltpu.roll(members[...], LANES - HALO, axis=1)[:, :own_rows]
    sums = jnp.dot(here, total, precision=lax.Precision.HIGHEST, preferred_element_type=f32)
    out[...] = jnp.concatenate([sums[j : j + 1] for j in range(GROUPS)], axis=1)


def join_kernel(own_rows, core, mine, pair, same, cross, skip, top, pooled):
    pair_rows = own_rows + HALO
    total = own_rows + 2 * HALO
    starts = (0, SKIP_HALO, SKIP_HALO + TOP_HALO)

    def put(rows, half, source):
        channels = slice(32 * half, 32 * (half + 1))
        narrow = slice(16 * half, 16 * (half + 1))
        here = slice(rows, rows + pair_rows)
        skip[here, channels] = source[:, :32]
        top[here, channels] = source[:, 32:64]
        pooled[here, narrow] = source[:, 64:80].astype(f32) + source[:, 80:96].astype(f32)

    def edge(above, half, source):
        channels = slice(32 * half, 32 * (half + 1))
        narrow = slice(16 * half, 16 * (half + 1))
        for out, count, start in ((skip, SKIP_HALO, starts[0]), (top, TOP_HALO, starts[1])):
            rows = HALO - count if above else pair_rows
            out[rows : rows + count, channels] = source[start : start + count]
            left = slice(0, rows) if above else slice(rows + count, total)
            out[left, channels] = jnp.zeros((HALO - count, 32, LANES), bf16)
        rows = 0 if above else pair_rows
        lines = source[starts[2] :].astype(f32)
        pooled[rows : rows + HALO, narrow] = lines[:, :16] + lines[:, 16:]

    @pl.when(core[0] == 0)
    def _():
        edge(True, 0, same)
        edge(True, 1, cross)
        put(HALO, 0, mine)
        put(HALO, 1, pair)

    @pl.when(core[0] == 1)
    def _():
        put(0, 0, pair)
        put(0, 1, mine)
        edge(False, 0, cross)
        edge(False, 1, same)


def gather_rows(kernel_out, perms):
    local, pair, same, cross = kernel_out
    return (
        local,
        lax.ppermute(pair, both, perms[0]),
        lax.ppermute(same, both, perms[1]),
        lax.ppermute(cross, both, perms[2]),
    )


CONVS = (
    ("first", 0), ("e0", 1), ("e1", 2), ("e2", 3), ("d0", 4), ("d1", 5), ("d2", 6), ("d3", 7)
)
NT = (((1,), (1,)), ((), ()))


def one_hot(height, width, offset):
    rows = lax.broadcasted_iota(jnp.int32, (height, width), 0)
    return (lanes_of((height, width)) == rows + offset).astype(f32).astype(bf16)


def piece_of(packed, which, index):
    if which in (0, 3):
        spot = 9 if which == 3 else 3 * index[0] + index[1]
        lane = 32 * (spot % 4)
        return packed[32 + spot // 4].astype(f32)[:, lane : lane + 32].astype(bf16)
    if which == 5:
        block = 35 + 2 * index[0]
        return jnp.concatenate([packed[block], packed[block + 1]], axis=1)
    spot = 63
    if which in (1, 2):
        spot = (0 if which == 1 else 27) + 9 * index[0] + 3 * index[1] + index[2]
    lane = 64 * (spot % 2)
    return packed[spot // 2].astype(f32)[:, lane : lane + 64].astype(bf16)


def prepare_kernel(core, stats, own, other, stats_copy, *refs):
    refs = list(refs)
    stats_copy[...] = stats[...]
    first = core[0] == 0
    mine, theirs = 32 * core[0], 32 * (1 - core[0])

    def whole(which, *index):
        left, right = piece_of(own, which, index), piece_of(other, which, index)
        return jnp.where(
            first,
            jnp.concatenate([left, right], axis=0),
            jnp.concatenate([right, left], axis=0),
        )

    def mixed(which, index, maker):
        return maker(piece_of(own, which, index), mine) + maker(
            piece_of(other, which, index), theirs
        )

    def put(width, lane):
        return lambda value, offset: dot(value, one_hot(32, width, lane + offset))

    rows_t = lax.broadcasted_iota(jnp.int32, (64, 32), 0)
    lanes_t = lanes_of((64, 32))

    def turn(value, offset):
        spot = (rows_t == lanes_t + offset).astype(f32).astype(bf16)
        return lax.dot_general(spot, value, NT, preferred_element_type=f32)

    ahead_all, back_all = refs.pop(0), refs.pop(0)
    ahead_all[...] = jnp.zeros_like(ahead_all)
    back_all[...] = jnp.zeros_like(back_all)
    back = back_all.at[0]
    for i in range(3):
        line = None
        span = None
        for j in range(3):
            term = mixed(0, (i, j), put(192, 64 * (2 - j)))
            line = term if line is None else line + term
            piece = dot(mixed(0, (i, j), turn).astype(bf16), one_hot(32, 96, 32 * j))
            span = piece if span is None else span + piece
        ahead_all[0, 64 * i : 64 * (i + 1), :96] = span.astype(bf16)
        back[32 * (2 - i) : 32 * (3 - i), :] = line.astype(bf16)
    eye = one_hot(64, 64, 0)
    empty = jnp.zeros((64, 64), bf16)
    for spot, (name, which, layer) in enumerate((
        ("e0", 1, 0), ("e1", 1, 1), ("e2", 1, 2),
        ("d0", 2, 0), ("d1", 2, 1), ("d2", 2, 2), ("d3", 2, 3),
    )):
        ahead, back = ahead_all.at[spot + 1], back_all.at[spot + 1]
        width = 256
        for i in range(3):
            taps = [whole(which, layer, i, j) for j in range(3)]
            span = None
            for j in range(3):
                piece = dot(taps[j], one_hot(64, width, 64 * j))
                span = piece if span is None else span + piece
            if i == 1 and name == "e0":
                turned = mixed(3, (Ellipsis,), turn).astype(bf16)
                span = span + dot(turned, one_hot(32, width, 192))
            if i == 1 and name == "d1":
                span = span + dot(whole(4, Ellipsis), one_hot(64, width, 192))
            ahead[64 * i : 64 * (i + 1), :] = span.astype(bf16)
            tall = jnp.concatenate([taps[2], taps[1], taps[0]], axis=0)
            back[64 * (2 - i) : 64 * (3 - i), :] = lax.dot_general(
                eye, tall, NT, preferred_element_type=f32
            ).astype(bf16)
        if name == "e0":
            back[192:224, :] = mixed(3, (Ellipsis,), put(192, 64)).astype(bf16)
        if name == "d1":
            tall = jnp.concatenate([empty, whole(4, Ellipsis), empty], axis=0)
            back[192:, :] = lax.dot_general(
                eye, tall, NT, preferred_element_type=f32
            ).astype(bf16)
    def small_of(packed):
        value = packed[41].astype(f32) + packed[42].astype(f32) + packed[43].astype(f32)
        tall = jnp.concatenate([value, jnp.zeros((LANES - 32, LANES), f32)], axis=0)
        return jnp.transpose(tall)

    flip_own, flip_other = small_of(own), small_of(other)

    def full(half):
        left, right = flip_own[:half], flip_other[:half]
        return jnp.where(
            first,
            jnp.concatenate([left, right], axis=0),
            jnp.concatenate([right, left], axis=0),
        )

    narrow, wide = full(16), full(32)
    small_norms, norms = refs.pop(0), refs.pop(0)
    for source, norm, gain, shift in (
        (narrow, small_norms.at[0], 0, 2), (narrow, small_norms.at[1], 1, 3),
        (wide, norms.at[0], 4, 7), (wide, norms.at[1], 5, 8), (wide, norms.at[2], 6, 9),
        (wide, norms.at[3], 10, 15), (wide, norms.at[4], 11, 16), (wide, norms.at[5], 12, 17),
        (wide, norms.at[6], 13, 18), (wide, norms.at[7], 14, 19),
    ):
        norm[0] = jnp.broadcast_to(source[:, gain : gain + 1], norm.shape[1:])
        norm[1] = jnp.broadcast_to(source[:, shift : shift + 1], norm.shape[1:])


def style_kernel(core, stats, counts, members, own, other, unit_out, *features):
    total = jnp.sum(stats[:, LANES:], axis=0, keepdims=True)
    channels = unit_out.shape[1]
    rows = lax.broadcasted_iota(jnp.int32, (8, channels), 0)
    sums = jnp.zeros((8, channels), f32)
    for j in range(GROUPS):
        piece = jnp.broadcast_to(total[:, channels * j : channels * (j + 1)], (8, channels))
        sums = sums + jnp.where(rows == j, piece, 0.0)
    means = sums / counts[:, :1]
    unit = means * lax.rsqrt(jnp.sum(means * means, axis=1, keepdims=True) + 1e-06)
    unit_out[...] = unit
    for layer, feature in enumerate(features):
        left = piece_of(own, 5, (layer,)).astype(f32)
        right = piece_of(other, 5, (layer,)).astype(f32)
        dense = jnp.where(
            core[0] == 0,
            jnp.concatenate([left, right], axis=0),
            jnp.concatenate([right, left], axis=0),
        )
        made = lax.dot_general(
            dense, unit, NT, precision=lax.Precision.HIGHEST, preferred_element_type=f32
        )
        out = jnp.zeros((64, LANES), f32)
        for j in range(GROUPS):
            out = out + made[:, j : j + 1] * members[j : j + 1, :]
        feature[...] = out


def input_grad_kernel(own_rows, inv_count, core, slope_a, slope_s, values, stats, sums, norms,
                      kept, sent):
    sums, norm_a, norm_s = [sums], norms.at[1], norms.at[0]
    center, scale = stats[0], stats[1]
    outer_s, col_s, const_s = back_columns(
        sums, 0, 32, 0, center, scale, norm_s[0], inv_count, 8
    )
    outer_a, col_a, const_a = back_columns(
        sums, 0, 32, 64, center, scale, norm_a[0], inv_count, 8
    )
    slope_col = col_s + col_a
    const_col = const_s + const_a
    first = core[0] == 0

    def body(step, carry):
        for k in range(4):
            row = 4 * step + k
            at = HALO + row
            grad = const_col - values[at] * slope_col
            grad = grad + slope_a[row + 2] * outer_a + slope_s[row + 2] * outer_s
            grad = (grad * 0.25).astype(bf16)
            low, high = grad[:16], grad[16:]
            kept[row] = jnp.where(first, low, high)
            sent[row] = jnp.where(first, high, low)
        return carry

    lax.fori_loop(0, own_rows // 4, body, 0)


def pixels_out_kernel(own_rows, core, kept, received, out, spread):
    home = pixel_home(lanes_of(spread.shape))
    rows = lax.broadcasted_iota(jnp.int32, spread.shape, 0)
    spread[...] = (home == rows).astype(f32).astype(bf16)
    wide = 4 * FULL_W
    half = own_rows // 2

    def body(step, carry):
        for which, source in enumerate((kept, received)):
            place = core[0] if which == 0 else 1 - core[0]
            left = jnp.concatenate(
                [
                    jnp.concatenate([source[8 * step + 2 * k], source[8 * step + 2 * k + 1]], axis=1)
                    for k in range(4)
                ],
                axis=0,
            )
            grown = dot(left, spread[...])
            for k in range(4):
                at = pl.multiple_of((place * half + 4 * step + k) * wide, LANES)
                out[:, pl.ds(at, wide)] = grown[16 * k : 16 * (k + 1)]
        return carry

    lax.fori_loop(0, own_rows // 8, body, 0)


def flat_kernel(own_rows, start, core, kept, received, out):
    lanes = lanes_of((32, LANES)).astype(f32).astype(bf16)

    def body(step, carry):
        for which, source in enumerate((kept, received)):
            place = core[0] if which == 0 else 1 - core[0]
            skip = 2 if which == 0 else start
            rows = [source[8 * step + k + skip] for k in range(8)]
            base = pl.multiple_of((place * own_rows + 8 * step) * POOL_W, LANES)
            for t in range(7):
                left = rows[t] if t == 0 else roll(rows[t], -16 * t)
                tile = jnp.where(
                    lanes < POOL_W - 16 * t, left, roll(rows[t + 1], POOL_W - 16 * t)
                )
                out[:, pl.ds(pl.multiple_of(base + LANES * t, LANES), LANES)] = tile.astype(f32)
        return carry

    lax.fori_loop(0, own_rows // 8, body, 0)


def pack_maps_kernel(own_rows, decoded, skip, out):
    def body(row, carry):
        out[row] = decoded[row + 2]
        out[own_rows + row] = skip[row + 2]
        return carry

    lax.fori_loop(0, own_rows, body, 0)


NAMES = ("d3", "d2", "d1", "d0", "e2", "e1", "e0", "first")
TILES = tuple((name, 0) for name in NAMES) + (
    ("d1", 1), ("e0", 1), ("d3", "d2"), ("d0", "e2"), ("e1", 1)
)
EXTRA = 16


def tile_of(parts, tile):
    name, which = tile
    if not isinstance(which, str):
        return parts[name][:, LANES * which : LANES * (which + 1)]
    left, right = parts[name][:, LANES:], parts[which][:, LANES:]
    return jnp.where(lanes_of(left.shape) < 64, left, pltpu.roll(right, 64, axis=1))


def split_two(value):
    upper = value.astype(bf16).astype(f32)
    return jnp.concatenate([upper, value - upper], axis=0).astype(bf16)


def sum_two(packed):
    value = packed.astype(f32)
    return value[:8] + value[8:]


def pack_grads_kernel(*refs):
    parts, stats, out = dict(zip(NAMES, refs[:-2])), refs[-2], refs[-1]
    for k, tile in enumerate(TILES):
        out[96 * k : 96 * (k + 1)] = tile_of(parts, tile).astype(bf16)
    out[96 * len(TILES) :] = split_two(stats[...])


def join_grads_kernel(per_strip, *refs):
    parts, stats, got, out = dict(zip(NAMES, refs[:-3])), refs[-3], refs[-2], refs[-1]
    chunk = per_strip + EXTRA
    strips = out.shape[0] // chunk
    at = 0
    for tile in TILES:
        value = (tile_of(parts, tile) + got[at : at + 96].astype(f32)).astype(bf16)
        for row in range(0, 96, 16):
            spot = at // per_strip * chunk + at % per_strip
            out[spot : spot + 16] = value[row : row + 16]
            at += 16
    lines = split_two(stats[...] + sum_two(got[at : at + 16]))
    for strip in range(strips):
        out[chunk * strip + per_strip : chunk * (strip + 1)] = lines
    while at < per_strip * strips:
        spot = at // per_strip * chunk + at % per_strip
        out[spot : spot + 16] = jnp.zeros((16, LANES), bf16)
        at += 16


def add_grads_kernel(per_strip, values, out, stats):
    chunk = per_strip + EXTRA
    strips = values.shape[0] // chunk
    total = values[:per_strip].astype(f32)
    lines = sum_two(values[per_strip:chunk])
    for k in range(1, strips):
        total = total + values[chunk * k : chunk * k + per_strip].astype(f32)
        lines = lines + sum_two(values[chunk * k + per_strip : chunk * (k + 1)])
    total = total.astype(bf16)
    stats[...] = lines
    for k in range(strips):
        out[per_strip * k : per_strip * (k + 1)] = total


def finish_kernel(seen, core, grads, unit, sp, sh0, se1, sh2, se2, *refs):
    refs = list(refs)
    su1, su2, su3 = [take(refs, count) for count in seen]
    (first_out, enc_out, eskip_out, in_gain, in_shift, enc_gain, enc_shift, dec_out, dskip_out,
     dec_gain, dec_shift, dense_out) = refs
    sp, sh0, se1, sh2, se2 = [sp], [sh0], [se1], [sh2], [se2]
    places = {}
    for k, (name, which) in enumerate(TILES):
        if isinstance(which, str):
            places[name, 1] = (k, 0)
            places[which, 1] = (k, 64)
        else:
            places[name, which] = (k, 0)

    def block(name, which):
        spot, lane = places[name, which]
        return grads[96 * spot : 96 * (spot + 1)].astype(f32), lane

    for refs, names in ((enc_out, ("e0", "e1", "e2")), (dec_out, ("d0", "d1", "d2", "d3"))):
        for k, name in enumerate(names):
            for i in range(3):
                source, lane = block(name, i // 2)
                lane = lane + 64 * (i % 2)
                for j in range(3):
                    refs[k, i, j] = source[32 * j : 32 * (j + 1), lane : lane + 64]
    tall = block("first", 0)[0]
    flipped = jnp.transpose(jnp.concatenate([tall, tall[:32]], axis=0))
    for j in range(3):
        for i in range(3):
            first_out[i, j] = flipped[32 * i : 32 * (i + 1), 32 * j : 32 * (j + 1)]
    tall = block("e0", 1)[0]
    flipped = jnp.transpose(jnp.concatenate([tall, tall[:32]], axis=0))
    eskip_out[...] = flipped[64:96, 32:64]
    dskip_out[...] = block("d1", 1)[0][32:64, 64:128]
    lines = [total_of(sp, 1 + k, 8) for k in range(6)]
    rows = lax.broadcasted_iota(jnp.int32, (LANES, LANES), 0)
    tall = jnp.zeros((LANES, LANES), f32)
    for k, line in enumerate(lines):
        tall = jnp.where(rows == k, jnp.broadcast_to(line, (LANES, LANES)), tall)
    flipped = jnp.transpose(tall)
    for layer in range(3):
        out = jnp.zeros((32, unit.shape[1]), f32)
        for j in range(GROUPS):
            at = 64 * (j % 2)
            column = slice(2 * layer + j // 2, 2 * layer + j // 2 + 1)
            picked = jnp.where(
                core[0] == 0, flipped[at : at + 32, column], flipped[at + 32 : at + 64, column]
            )
            out = out + picked * unit[j : j + 1, :]
        dense_out[layer] = out

    def pick(stats, slot, lane, half, period=1):
        total = total_of(stats, slot, period)
        low = total[:1, lane : lane + half]
        high = total[:1, lane + half : lane + 2 * half]
        return jnp.where(core[0] == 0, low, high)

    for k in range(2):
        in_shift[k : k + 1, :] = pick(sp, 0, 64 * k, 16, 8)
        in_gain[k : k + 1, :] = pick(sp, 0, 64 * k + 32, 16, 8)
    for k, stats in enumerate((sh0, se1, sh2)):
        enc_shift[k : k + 1, :] = pick(stats, 0, 0, 32)
        enc_gain[k : k + 1, :] = pick(stats, 0, 64, 32)
    for k, (stats, slot) in enumerate(((se2, 0), (se2, 1), (su1, 0), (su2, 0), (su3, 0))):
        dec_shift[k : k + 1, :] = pick(stats, slot, 0, 32, 2 if stats is se2 else 1)
        dec_gain[k : k + 1, :] = pick(stats, slot, 64, 32, 2 if stats is se2 else 1)


def pixel_home(index):
    upper = (index >= 2 * FULL_W).astype(jnp.int32)
    line = index - 2 * FULL_W * upper
    column = line - FULL_W * (line >= FULL_W).astype(jnp.int32)
    return LANES * upper + column // 2


def share(values):
    return (lax.all_to_all(values, both, 0, 0, tiled=True),)


def per_device(
    pixels, skip_map, style_map, crop_rows, crop_group, enc_first, enc_convs, enc_skip,
    enc_in_gain, enc_in_shift, enc_gain, enc_shift, dec_convs, dec_skip, dec_gain, dec_shift,
    dense, out_grad,
):
    strip_rows = skip_map.shape[1] // POOL_W
    own = strip_rows // 2
    strips = lax.axis_size("rows")
    devices = 2 * strips
    inv_count = 1.0 / (strips * strip_rows * POOL_W)
    core_index = lax.axis_index("ch").astype(jnp.int32)
    core = core_index[None]
    total = own + 2 * HALO
    place = (lax.axis_index("rows").astype(jnp.int32) * strip_rows + core_index * own)[None]
    swap = [(i, i ^ 1) for i in range(devices)]
    same = []
    cross = []
    for i in range(strips - 1):
        same += [(2 * i, 2 * i + 2), (2 * i + 3, 2 * i + 1)]
        cross += [(2 * i + 1, 2 * i + 2), (2 * i + 2, 2 * i + 1)]
    perms = (swap, same, cross)
    pair_rows = own + HALO

    def turned(value):
        return jnp.swapaxes(value, -1, -2)

    packed, _ = call(
        pack_kernel, "pack",
        [(value, False) for value in
         (enc_first, turned(enc_convs), turned(dec_convs), enc_skip, turned(dec_skip),
          turned(dense), enc_in_gain, enc_in_shift, enc_gain, enc_shift, dec_gain, dec_shift)],
        [((44, 32, LANES), bf16), ((32, LANES), f32)], cost=1,
    )
    packed_other = lax.ppermute(packed, both, swap)
    *made, stats_p = call(
        functools.partial(entry_kernel, own), "entry",
        [(core, True), (skip_map, "hbm"), (out_grad, "hbm"), (pixels, "hbm")],
        [
            ((pair_rows, 96, LANES), bf16, "hbm"), ((pair_rows, 96, LANES), bf16, "hbm"),
            ((SKIP_HALO + TOP_HALO + HALO, 32, LANES), bf16, "hbm"),
            ((SKIP_HALO + TOP_HALO + HALO, 32, LANES), bf16, "hbm"), ((devices, LANES), f32),
        ],
        [pltpu.VMEM((2, 16, LANES), f32)]
        + [pltpu.VMEM(value.shape, bf16) for value in (skip_map, out_grad, pixels)]
        + [pltpu.VMEM((4 * FULL_W, 2 * LANES), bf16), pltpu.VMEM((strip_rows, 64, LANES), bf16)]
        + [pltpu.VMEM((strip_rows, 32, LANES), bf16)]
        + [pltpu.SemaphoreType.DMA((3,)), pltpu.SemaphoreType.DMA((10,))],
        limit=60,
    )
    map_parts = gather_rows(made, perms)
    meta, members, counts = call(
        functools.partial(crop_kernel, own, strip_rows, style_map.shape[1]), "crops",
        [(place, True), (crop_rows, True), (crop_group, True)],
        [((8, LANES), jnp.int32), ((8, LANES), f32), ((8, LANES), f32)], cost=1,
    )
    (style_sums,) = call(
        functools.partial(style_sum_kernel, own), "style_sums",
        [(core, True), (jnp.swapaxes(style_map, 0, 1), False), (members, False)],
        [((1, GROUPS * style_map.shape[2]), f32)], cost=1,
    )
    stats_p, ahead, back, norms_in, norms = call(
        prepare_kernel, "prepare",
        [(core, True), (stats_p, False), (packed, False), (packed_other, False)],
        [
            ((devices, LANES), f32),
            ((8, 192, 256), bf16), ((8, 256, 192), bf16),
            ((2, 2, 32, LANES), f32), ((8, 2, 64, LANES), f32),
        ],
        after=(style_sums,),
    )
    stats_p = share(stats_p)
    skip_full, top_full, pooled = call(
        functools.partial(join_kernel, own), "join",
        [(core, True)] + [(part, False) for part in map_parts],
        [((total, 64, LANES), bf16), ((total, 64, LANES), bf16), ((total, 32, LANES), f32)],
        after=stats_p,
    )

    go = functools.partial(
        forward, keep=meta, norms=norms, weights=ahead, own_rows=own, inv_count=inv_count,
        out_rows=devices,
    )
    h0, a0, s0, c_p, t_h0 = go(
        "ahead_h0", values=pooled, stats=stats_p, norms=norms_in, spots=(1, 0), layer=0, f=13,
        after=(top_full,),
    )
    t_h0 = share(t_h0)
    e1, a1, c_h0, t_e1 = go(
        "ahead_e1", values=h0, stats=t_h0, spots=(0,), layer=1, f=12, skip_in=s0,
        payload=style_sums,
    )
    t_e1 = share(t_e1)
    unit, *feature = call(
        style_kernel, "style",
        [(core, True), (t_e1[0], False), (counts, False), (members, False), (packed, False),
         (packed_other, False)],
        [((8, style_map.shape[2]), f32)] + [((64, LANES), f32)] * 3, cost=1,
    )
    h2, a2, c_e1, t_h2 = go(
        "ahead_h2", values=e1, stats=t_e1, spots=(1,), layer=2, f=11, after=(unit,)
    )
    t_h2 = share(t_h2)
    e2, a3, c_h2, t_e2 = go(
        "ahead_e2", values=h2, stats=t_h2, spots=(2,), layer=3, f=10, residual=e1
    )
    t_e2 = share(t_e2)
    u1, b0, q0, c_e2, t_u1 = go(
        "ahead_u1", values=e2, stats=t_e2, spots=(4, 3), layer=4, f=9, skip_map=skip_full,
        feature=feature[0],
    )
    t_u1 = share(t_u1)
    u2, raw_d1, b1, c_u1, t_u2 = go(
        "ahead_u2", values=u1, stats=t_u1, spots=(5,), layer=5, f=8, skip_in=q0,
        skip_map=skip_full, feature=feature[1], keep_raw=True,
    )
    t_u2 = share(t_u2)
    u3, b2, c_u2, t_u3 = go(
        "ahead_u3", values=u2, stats=t_u2, spots=(6,), layer=6, f=7, feature=feature[2]
    )
    t_u3 = share(t_u3)
    ret = functools.partial(
        backward, keep=meta, core=core, norms=norms, below_norms=norms, weights=back,
        own_rows=own, inv_count=inv_count, out_rows=devices,
    )
    parts = {}
    slope_u3, s_u3, *parts["d3"], sums_top, b3, c_u3 = ret(
        "back_top", slopes=[], values=None, stats=None, sums=(), spots=(), layer=7, below=u3,
        below_stats=t_u3[0], below_spot=7, act=None, b=8, extra=top_full, export=True,
    )
    s_u3 = share(s_u3)
    slope_u2, s_u2, *parts["d2"], sums_u3 = ret(
        "back_u3", slopes=[slope_u3], values=u3, stats=c_u3, sums=s_u3, spots=(7,), layer=6,
        below=u2, below_stats=c_u2, below_spot=6, act=b2, b=7, export=True,
    )
    s_u2 = share(s_u2)
    pure_u2, slope_u1, slope_q0, s_u1, *parts["d1"], sums_d1 = ret(
        "back_u2", slopes=[slope_u2], values=u2, stats=c_u2, sums=s_u2, spots=(6,), layer=5,
        below=u1, below_stats=c_u1, below_spot=5, act=b1, b=6, extra=top_full, extra_rows=64,
        save="own", skip_in=q0, export=True,
    )
    s_u1 = share(s_u1)
    slope_b0, skip_kept, skip_sent, s_e2, *parts["d0"], sums_u1 = ret(
        "back_u1", slopes=[slope_u1], values=u1, stats=c_u1, sums=s_u1, spots=(5,), layer=4,
        below=e2, below_stats=c_e2, below_spot=4, act=b0, b=5, below_side=slope_q0,
        other=pure_u2, export=True,
    )
    s_e2 = share(s_e2)
    pure_e2, slope_h2, s_h2, *parts["e2"] = ret(
        "back_e2", slopes=[slope_q0, slope_b0], values=e2, stats=c_e2, sums=s_e2, spots=(3, 4),
        layer=3, below=h2, below_stats=c_h2, below_spot=2, act=a3, b=4, save="all",
    )
    s_h2 = share(s_h2)
    slope_e1, s_e1, *parts["e1"] = ret(
        "back_h2", slopes=[slope_h2], values=h2, stats=c_h2, sums=s_h2, spots=(2,), layer=2,
        below=e1, below_stats=c_e1, below_spot=1, act=a2, b=3,
    )
    s_e1 = share(s_e1)
    slope_h0, slope_s0, s_h0, *parts["e0"] = ret(
        "back_e1", slopes=[slope_e1], values=e1, stats=c_e1, sums=s_e1, spots=(1,), layer=1,
        below=h0, below_stats=c_h0, below_spot=0, act=a1, b=2, extra=pure_e2, extra_rows=32,
        skip_in=s0,
    )
    s_h0 = share(s_h0)
    slope_a0, s_p, *parts["first"] = ret(
        "back_h0", slopes=[slope_h0], values=h0, stats=c_h0, sums=s_h0, spots=(0,), layer=0,
        below=pooled, below_stats=c_p, below_norms=norms_in, below_spot=1, act=a0, b=1,
        below_side=slope_s0, gathered=(sums_top, sums_u3, sums_d1, sums_u1),
    )
    tall = 96 * len(TILES)
    per_strip = -(-tall // (16 * strips)) * 16
    (sent,) = call(
        pack_grads_kernel, "pack_grads",
        [(parts[name][1], False) for name in NAMES] + [(s_p, False)],
        [((tall + EXTRA, LANES), bf16)], cost=1,
    )
    got = lax.ppermute(sent, both, swap)
    (joined,) = call(
        functools.partial(join_grads_kernel, per_strip), "join_grads",
        [(parts[name][0], False) for name in NAMES] + [(s_p, False), (got, False)],
        [(((per_strip + EXTRA) * strips, LANES), bf16)], cost=1,
    )
    scattered = lax.all_to_all(joined, "rows", 0, 0, tiled=True)
    decoded_kept, decoded_sent = call(
        functools.partial(decode_kernel, own), "decode",
        [(meta, True), (core, True), (b3, False), (ahead, False), (raw_d1, False)],
        [((own + 4, 32, LANES), bf16), ((own + 4, 32, LANES), bf16)],
        [pltpu.VMEM((2, 64, LANES), f32)], after=(s_p,),
    )
    (maps_sent,) = call(
        functools.partial(pack_maps_kernel, own), "pack_maps",
        [(decoded_sent, False), (skip_sent, False)],
        [((2 * own, 32, LANES), bf16)], cost=0.1,
    )
    maps_got = lax.ppermute(maps_sent, both, swap)
    (skip_grad,) = call(
        functools.partial(flat_kernel, own, own), "flat_skip",
        [(core, True), (skip_kept, False), (maps_got, False)],
        [((32, strip_rows * POOL_W), f32)], limit=60, cost=0.2,
    )
    (decoded,) = call(
        functools.partial(flat_kernel, own, 0), "flat_decoded",
        [(core, True), (decoded_kept, False), (maps_got, False)],
        [((32, strip_rows * POOL_W), f32)], limit=60, cost=0.2,
    )
    added, s_p = call(
        functools.partial(add_grads_kernel, per_strip), "add_grads", [(scattered, False)],
        [((per_strip * strips, LANES), bf16), ((8, LANES), f32)], limit=60, cost=1,
        after=(skip_grad, decoded),
    )
    grads = lax.all_to_all(added, "rows", 0, 0, tiled=True)
    pix_kept, pix_sent = call(
        functools.partial(input_grad_kernel, own, inv_count), "back_pooled",
        [(core, True), (slope_a0, False), (slope_s0, False), (pooled, False),
         (c_p, False), (s_p, False), (norms_in, False)],
        [((own, 16, LANES), bf16), ((own, 16, LANES), bf16)], cost=1,
    )
    pix_got = lax.ppermute(pix_sent, both, swap)
    (pixels_grad,) = call(
        functools.partial(pixels_out_kernel, own), "pixels_out",
        [(core, True), (pix_kept, False), (pix_got, False)],
        [((16, 4 * strip_rows * POOL_W), f32)],
        [pltpu.VMEM((2 * LANES, 4 * FULL_W), bf16)], limit=10, cost=0.5,
    )
    outs = [
        ((3, 3, 32, 32), f32), ((3, 3, 3, 32, 64), f32), ((32, 32), f32), ((2, 16), f32),
        ((2, 16), f32), ((3, 32), f32), ((3, 32), f32), ((4, 3, 3, 32, 64), f32), ((32, 64), f32),
        ((5, 32), f32), ((5, 32), f32), ((3, 32, style_map.shape[2]), f32),
    ]
    (s_h0,), (s_e1,), (s_h2,), (s_e2,) = s_h0, s_e1, s_h2, s_e2
    rest = call(
        functools.partial(finish_kernel, (len(s_u1), len(s_u2), len(s_u3))), "finish",
        [(core, True), (grads, False)]
        + [(value, False)
           for value in (unit, s_p, s_h0, s_e1, s_h2, s_e2, *s_u1, *s_u2, *s_u3)],
        outs, limit=8,
    )
    rest = list(rest)
    for spot in (1, 7, 8, 11):
        rest[spot] = turned(rest[spot])
    return (decoded, pixels_grad, skip_grad) + tuple(rest)


def solution(mesh):
    placed = (
        P("ch", "rows"),
        P("ch", "rows"),
        P("rows", None, None),
        P(),
        P(),
        P(None, None, None, "ch"),
        P(None, None, None, None, "ch"),
        P(None, "ch"),
        P(None, "ch"),
        P(None, "ch"),
        P(None, "ch"),
        P(None, "ch"),
        P(None, None, None, None, "ch"),
        P(None, "ch"),
        P(None, "ch"),
        P(None, "ch"),
        P(None, None, "ch"),
        P("ch", "rows"),
    )
    return jax.shard_map(
        per_device,
        mesh=mesh,
        in_specs=placed,
        out_specs=(
            P("ch", "rows"),
            P("ch", "rows"),
            P("ch", "rows"),
            P(None, None, None, "ch"),
            P(None, None, None, None, "ch"),
            P(None, "ch"),
            P(None, "ch"),
            P(None, "ch"),
            P(None, "ch"),
            P(None, "ch"),
            P(None, None, None, None, "ch"),
            P(None, "ch"),
            P(None, "ch"),
            P(None, "ch"),
            P(None, None, "ch"),
        ),
        check_vma=False,
    )
```

time: 2150 us -> 268 us (0.12)
  local copies, waits for them, and re-layouts: 796 us -> 4.53 us
  blocking collectives: 729 us -> 125 us
  other arithmetic: 251 us -> 0 us
  matrix products: 177 us -> 0 us
  Pallas kernels: 0 us -> 96.9 us
  waiting for transfers between devices: 86.3 us -> 17.5 us
  starting transfers between devices: 72.5 us -> 21.5 us
    psum x16 -> x0, blocking collectives: 723 us -> none  [the longest x8 367 us: statistics(): return settle(lax.psum(moments(values), 'rows'), pixel_count)]
    reshape x24 -> x0, local copies, waits for them, and re-layouts: 338 us -> none  [the longest x8 267 us: patches(): return jnp.concatenate(pieces, axis=2).reshape(strip_rows * pool_width, -1)]
    concatenate x24 -> x0, local copies, waits for them, and re-layouts: 191 us -> none  [patches(): return jnp.concatenate(pieces, axis=2).reshape(strip_rows * pool_width, -1)]
    dot_general x46 -> x0, matrix products: 177 us -> none  [the longest x8 78.5 us: conv_back(): lax.dot_general(forward_cols, rounded.reshape(strip_rows * pool_width, ou...]
    reduce_sum x15 -> x0, other arithmetic: 128 us -> none  [the longest x1 80.4 us: per_device(): jnp.mean(full_res.reshape(strip_rows, 2, pool_width, 2, full_res.shape[2]...]
    all_to_all x0 -> x14, blocking collectives: none -> 125 us  [share(): return (lax.all_to_all(values, both, 0, 0, tiled=True),)]
    unnamed x415 -> x83, local copies, waits for them, and re-layouts: 104 us -> 4.38 us
    pallas_call x0 -> x32, Pallas kernels: none -> 96.9 us  [call(): pl.pallas_call(body, name=name, out_shape=tuple((jax.ShapeDtypeStruct(out...]
  transfers between devices with their start and end apart: 51 -> 10, of which waited for: 17 -> 4; matrix products, arithmetic and copies ran while one was open for 41% -> 0% of each run, Pallas kernels for 0% -> 7%
where the time goes in v1:
time: 268 us; the launch traced here: 267 us
  blocking collectives  125 us (47%)
  Pallas kernels  96.9 us (36%)
  starting transfers between devices  21.5 us (8%)
  waiting for transfers between devices  17.5 us (7%)
  local copies, waits for them, and re-layouts  4.53 us (2%)
    all_to_all x14, blocking collectives, share(): return (lax.all_to_all(values, both, 0, 0, tiled=True),)  125 us
    pallas_call x32, Pallas kernels, call(): pl.pallas_call(body, name=name, out_shape=tuple((jax.ShapeDtypeStruct(out...  96.9 us
    all_to_all x1, waiting for transfers between devices, share(): return (lax.all_to_all(values, both, 0, 0, tiled=True),)  7.05 us
    all_to_all x1, starting transfers between devices, share(): return (lax.all_to_all(values, both, 0, 0, tiled=True),)  6.67 us
    all_to_all x1, waiting for transfers between devices, per_device(): scattered = lax.all_to_all(joined, 'rows', 0, 0, tiled=True)  6.25 us
  transfers between devices with their start and end apart: 10, of which 4 were waited for; matrix products, arithmetic and copies ran while one was open for 0% of the time, Pallas kernels for 7%

profile of v1, /device:TPU:0, one launch (start us, length us, event | category | flops | bytes accessed | tf_op | source)
XLA Modules:
  0.0 267.1 jit_solution(9369132906201893177)
XLA Ops:
  0.8 7.5 %entry.1 = (bf16[78,96,128]{2,1,0:T(8,128)(2,1)}, bf16[78,96,128]{2,1,0:T(8,128)(2,1)}, bf16[31,32,128]{2,1,0:T(8,128)(2,1)}, bf16[31,32,128]{2,1,0:T(8,128)(2,1)}, f32[32,128]{1,0:T(8,128)}) custom-call(s32[1]{0:T(128)} %bitcast.refs_0_.refs_1_, bf16[32,14336]{1,0:T(8,128)(2,1)} %refs_1_.3, bf16[32,14336]{1,0:T(8,128)(2,1)} %refs_2_.3, ...), custom_call_target="tpu_custom_call" | custom-call | bytes 14000000 | tf_op jit(solution)/shard_map/entry/pallas_call | solution.py:39
  8.3 0.5 collective-permute-start
  8.9 0.7 pack.1
  9.7 4.8 %collective-permute-start.1 = (bf16[31,32,128]{2,1,0:T(8,128)(2,1)}, bf16[31,32,128]{2,1,0:T(8,128)(2,1)S(1)}, u32[]{:S(2)}, u32[]{:S(2)}) collective-permute-start(bf16[31,32,128]{2,1,0:T(8,128)(2,1)} %get-tuple-element.132), channel_id=1, source_target_pairs={{0,2},{3,1},{2,4},{5,3},{4,6},{7,5},{6,8},{9,7},{8,10},{11,9},{10,... | collective-permute-start | bytes 761864 | tf_op jit(solution)/shard_map/ppermute | solution.py:809
  14.5 1.4 collective-permute-start.2
  15.9 0.6 crops.1
  16.5 0.3 style_sums.1.refs_4_.refs_6_
  16.8 2.5 prepare.1
  19.3 6.7 %all-to-all-start = ((f32[32,1,128]{2,1,0:T(1,128)}), f32[32,1,128]{2,1,0:T(1,128)S(1)}, u32[]{:S(2)}, u32[]{:S(2)}) async-start(f32[32,1,128]{2,1,0:T(1,128)} %bitcast.8), calls=%async_computation | async-start | bytes 32768 | tf_op jit(solution)/shard_map/all_to_all | solution.py:1195
  26.0 7.1 %all-to-all-done = f32[32,1,128]{2,1,0:T(1,128)S(1)} async-done(((f32[32,1,128]{2,1,0:T(1,128)}), f32[32,1,128]{2,1,0:T(1,128)S(1)}, u32[]{:S(2)}, u32[]{:S(2)}) %all-to-all-start) | async-done | bytes 16416 | tf_op jit(solution)/shard_map/all_to_all | solution.py:1195
  33.0 1.5 copy-done.2
  34.6 1.9 join.1
  36.5 2.9 %ahead_h0.1 = (f32[92,64,128]{2,1,0:T(8,128)S(1)}, bf16[68,32,128]{2,1,0:T(8,128)(2,1)S(1)}, bf16[92,32,128]{2,1,0:T(8,128)(2,1)S(1)}, f32[2,32,128]{2,1,0:T(8,128)S(1)}, f32[32,128]{1,0:T(8,128)S(1)}) custom-call(s32[8,128]{1,0:T(8,128)S(1)} %get-tuple-element.129.refs_0_, f32[92,32,128]{2,1,0:T(8,128)S(1)} %get-tuple-element.140.refs_1_.refs_8_.refs_3_, ...), custom_call_target="tpu_custom_call" | custom-call | bytes 14000000 | tf_op jit(solution)/shard_map/ahead_h0/pallas_call | solution.py:39
  39.4 8.8 %all_to_all.187 = f32[32,1,128]{2,1,0:T(1,128)S(1)} all-to-all(f32[32,1,128]{2,1,0:T(1,128)S(1)} %bitcast.112), channel_id=1, replica_groups=mesh['rows'=16,'ch'=2] {'rows','ch'}, dimensions={0} | all-to-all | bytes 32768 | tf_op jit(solution)/shard_map/all_to_all | solution.py:1195
  48.2 3.0 %ahead_e1.1 = (f32[92,64,128]{2,1,0:T(8,128)S(1)}, bf16[68,64,128]{2,1,0:T(8,128)(2,1)S(1)}, f32[2,64,128]{2,1,0:T(8,128)S(1)}, f32[32,1152]{1,0:T(8,128)S(1)}) custom-call(s32[8,128]{1,0:T(8,128)S(1)} %get-tuple-element.129.refs_0_, f32[92,64,128]{2,1,0:T(8,128)S(1)} %get-tuple-element.143.refs_1_.refs_9_.refs_3_, f32[32,128]{1,0:T(8,128)S(1)} %bitcast.100, ...), custom_call_target="tpu_custom_call" | custom-call | bytes 14000000 | tf_op jit(solution)/shard_map/ahead_e1/pallas_call | solution.py:39
  51.2 0.2 copy.35
  51.4 10.1 %all_to_all.188 = f32[32,1,1152]{2,1,0:T(1,128)S(1)} all-to-all(f32[32,1,1152]{2,1,0:T(1,128)S(1)} %copy.35), channel_id=1, replica_groups=mesh['rows'=16,'ch'=2] {'rows','ch'}, dimensions={0} | all-to-all | bytes 294912 | tf_op jit(solution)/shard_map/all_to_all | solution.py:1195
  61.5 0.6 style.1
  62.1 3.0 %ahead_h2.1 = (f32[92,64,128]{2,1,0:T(8,128)S(1)}, bf16[68,64,128]{2,1,0:T(8,128)(2,1)S(1)}, f32[2,64,128]{2,1,0:T(8,128)S(1)}, f32[32,128]{1,0:T(8,128)S(1)}) custom-call(s32[8,128]{1,0:T(8,128)S(1)} %get-tuple-element.129.refs_0_, f32[92,64,128]{2,1,0:T(8,128)S(1)} %get-tuple-element.147.refs_1_.refs_5_.refs_8_.refs_3_, f32[32,1152]{1,0:T(8,128)S(1)} %bitcast.75, ...), custom_call_target="tpu_custom_call" | custom-call | bytes 14000000 | tf_op jit(solution)/shard_map/ahead_h2/pallas_call | solution.py:39
  65.1 9.0 %all_to_all.189 = f32[32,1,128]{2,1,0:T(1,128)S(1)} all-to-all(f32[32,1,128]{2,1,0:T(1,128)S(1)} %bitcast.114), channel_id=1, replica_groups=mesh['rows'=16,'ch'=2] {'rows','ch'}, dimensions={0} | all-to-all | bytes 32768 | tf_op jit(solution)/shard_map/all_to_all | solution.py:1195
  74.1 3.2 %ahead_e2.1 = (f32[92,64,128]{2,1,0:T(8,128)S(1)}, bf16[68,64,128]{2,1,0:T(8,128)(2,1)S(1)}, f32[2,64,128]{2,1,0:T(8,128)S(1)}, f32[32,128]{1,0:T(8,128)S(1)}) custom-call(s32[8,128]{1,0:T(8,128)S(1)} %get-tuple-element.129.refs_0_, f32[92,64,128]{2,1,0:T(8,128)S(1)} %get-tuple-element.151.refs_1_.refs_9_.refs_3_, f32[32,128]{1,0:T(8,128)S(1)} %bitcast.101, ...), custom_call_target="tpu_custom_call" | custom-call | bytes 14000000 | tf_op jit(solution)/shard_map/ahead_e2/pallas_call | solution.py:39
  77.3 8.8 %all_to_all.190 = f32[32,1,128]{2,1,0:T(1,128)S(1)} all-to-all(f32[32,1,128]{2,1,0:T(1,128)S(1)} %bitcast.115), channel_id=1, replica_groups=mesh['rows'=16,'ch'=2] {'rows','ch'}, dimensions={0} | all-to-all | bytes 32768 | tf_op jit(solution)/shard_map/all_to_all | solution.py:1195
  86.1 3.6 %ahead_u1.1 = (f32[92,64,128]{2,1,0:T(8,128)S(1)}, bf16[68,64,128]{2,1,0:T(8,128)(2,1)S(1)}, bf16[92,64,128]{2,1,0:T(8,128)(2,1)S(1)}, f32[2,64,128]{2,1,0:T(8,128)S(1)}, f32[32,128]{1,0:T(8,128)S(1)}) custom-call(s32[8,128]{1,0:T(8,128)S(1)} %get-tuple-element.129.refs_0_, f32[92,64,128]{2,1,0:T(8,128)S(1)} %get-tuple-element.153.refs_1_.refs_8_.refs_4_, ...), custom_call_target="tpu_custom_call" | custom-call | bytes 14000000 | tf_op jit(solution)/shard_map/ahead_u1/pallas_call | solution.py:39
  89.8 8.8 %all_to_all.191 = f32[32,1,128]{2,1,0:T(1,128)S(1)} all-to-all(f32[32,1,128]{2,1,0:T(1,128)S(1)} %bitcast.111), channel_id=1, replica_groups=mesh['rows'=16,'ch'=2] {'rows','ch'}, dimensions={0} | all-to-all | bytes 32768 | tf_op jit(solution)/shard_map/all_to_all | solution.py:1195
  98.6 3.5 %ahead_u2.1 = (f32[92,64,128]{2,1,0:T(8,128)S(1)}, f32[68,64,128]{2,1,0:T(8,128)S(1)}, bf16[68,64,128]{2,1,0:T(8,128)(2,1)S(1)}, f32[2,64,128]{2,1,0:T(8,128)S(1)}, f32[32,128]{1,0:T(8,128)S(1)}) custom-call(s32[8,128]{1,0:T(8,128)S(1)} %get-tuple-element.129.refs_0_, f32[92,64,128]{2,1,0:T(8,128)S(1)} %get-tuple-element.157.refs_1_.refs_9_.refs_3_, ...), custom_call_target="tpu_custom_call" | custom-call | bytes 14000000 | tf_op jit(solution)/shard_map/ahead_u2/pallas_call | solution.py:39
  102.1 8.8 %all_to_all.192 = f32[32,1,128]{2,1,0:T(1,128)S(1)} all-to-all(f32[32,1,128]{2,1,0:T(1,128)S(1)} %bitcast.108), channel_id=1, replica_groups=mesh['rows'=16,'ch'=2] {'rows','ch'}, dimensions={0} | all-to-all | bytes 32768 | tf_op jit(solution)/shard_map/all_to_all | solution.py:1195
  111.0 3.0 %ahead_u3.1 = (f32[92,64,128]{2,1,0:T(8,128)S(1)}, bf16[68,64,128]{2,1,0:T(8,128)(2,1)S(1)}, f32[2,64,128]{2,1,0:T(8,128)S(1)}, f32[32,128]{1,0:T(8,128)S(1)}) custom-call(s32[8,128]{1,0:T(8,128)S(1)} %get-tuple-element.129.refs_0_, f32[92,64,128]{2,1,0:T(8,128)S(1)} %get-tuple-element.161.refs_1_.refs_8_.refs_3_, f32[32,128]{1,0:T(8,128)S(1)} %bitcast.99, ...), custom_call_target="tpu_custom_call" | custom-call | bytes 14000000 | tf_op jit(solution)/shard_map/ahead_u3/pallas_call | solution.py:39
  114.0 8.8 %all_to_all.193 = f32[32,1,128]{2,1,0:T(1,128)S(1)} all-to-all(f32[32,1,128]{2,1,0:T(1,128)S(1)} %bitcast.113), channel_id=1, replica_groups=mesh['rows'=16,'ch'=2] {'rows','ch'}, dimensions={0} | all-to-all | bytes 32768 | tf_op jit(solution)/shard_map/all_to_all | solution.py:1195
  122.9 6.2 %back_top.1 = (f32[92,64,128]{2,1,0:T(8,128)S(1)}, f32[32,128]{1,0:T(8,128)S(1)}, f32[96,256]{1,0:T(8,128)S(1)}, f32[96,256]{1,0:T(8,128)S(1)}, f32[8,128]{1,0:T...) custom-call(s32[8,128]{1,0:T(8,128)S(1)} %get-tuple-element.129.refs_0_, ...), custom_call_target="tpu_custom_call" | custom-call | bytes 14000000 | tf_op jit(solution)/shard_map/back_top/pallas_call | solution.py:39
  129.1 8.8 %all_to_all.194 = f32[32,1,128]{2,1,0:T(1,128)S(1)} all-to-all(f32[32,1,128]{2,1,0:T(1,128)S(1)} %bitcast.109), channel_id=1, replica_groups=mesh['rows'=16,'ch'=2] {'rows','ch'}, dimensions={0} | all-to-all | bytes 32768 | tf_op jit(solution)/shard_map/all_to_all | solution.py:1195
  137.9 5.5 %back_u3.1 = (f32[92,64,128]{2,1,0:T(8,128)S(1)}, f32[32,128]{1,0:T(8,128)S(1)}, f32[96,256]{1,0:T(8,128)S(1)}, f32[96,256]{1,0:T(8,128)S(1)}, f32[8,128]{1,0:T(8,128)S(1)}) custom-call(s32[8,128]{1,0:T(8,128)S(1)} %get-tuple-element.129.refs_0_, s32[1]{0:T(128)} %bitcast.refs_0_.refs_1_, f32[92,64,128]{2,1,0:T(8,128)S(1)} %get-tuple-element.168.refs_2_, ...), custom_call_target="tpu_custom_call" | custom-call | bytes 14000000 | tf_op jit(solution)/shard_map/back_u3/pallas_call | solution.py:39
  143.4 8.8 %all_to_all.195 = f32[32,1,128]{2,1,0:T(1,128)S(1)} all-to-all(f32[32,1,128]{2,1,0:T(1,128)S(1)} %bitcast.107), channel_id=1, replica_groups=mesh['rows'=16,'ch'=2] {'rows','ch'}, dimensions={0} | all-to-all | bytes 32768 | tf_op jit(solution)/shard_map/all_to_all | solution.py:1195
  152.3 6.1 %back_u2.1 = (f32[68,64,128]{2,1,0:T(8,128)S(1)}, f32[92,64,128]{2,1,0:T(8,128)S(1)}, f32[92,64,128]{2,1,0:T(8,128)S(1)}, f32[32,128]{1,0:T(8,128)S(1)}, f32[96,...) custom-call(s32[8,128]{1,0:T(8,128)S(1)} %get-tuple-element.129.refs_0_, s32[1]{0:T(128)} %bitcast.refs_0_.refs_1_, ...), custom_call_target="tpu_custom_call" | custom-call | bytes 14000000 | tf_op jit(solution)/shard_map/back_u2/pallas_call | solution.py:39
  158.4 8.8 %all_to_all.196 = f32[32,1,128]{2,1,0:T(1,128)S(1)} all-to-all(f32[32,1,128]{2,1,0:T(1,128)S(1)} %bitcast.104), channel_id=1, replica_groups=mesh['rows'=16,'ch'=2] {'rows','ch'}, dimensions={0} | all-to-all | bytes 32768 | tf_op jit(solution)/shard_map/all_to_all | solution.py:1195
  167.3 6.0 %back_u1.1 = (f32[92,64,128]{2,1,0:T(8,128)S(1)}, bf16[68,32,128]{2,1,0:T(8,128)(2,1)S(1)}, bf16[68,32,128]{2,1,0:T(8,128)(2,1)S(1)}, f32[64,128]{1,0:T(8,128)S(...) custom-call(s32[8,128]{1,0:T(8,128)S(1)} %get-tuple-element.129.refs_0_, ...), custom_call_target="tpu_custom_call" | custom-call | bytes 14000000 | tf_op jit(solution)/shard_map/back_u1/pallas_call | solution.py:39
  173.4 8.9 %all_to_all.197 = f32[32,2,128]{2,1,0:T(2,128)S(1)} all-to-all(f32[32,2,128]{2,1,0:T(2,128)S(1)} %bitcast.103), channel_id=1, replica_groups=mesh['rows'=16,'ch'=2] {'rows','ch'}, dimensions={0} | all-to-all | bytes 65536 | tf_op jit(solution)/shard_map/all_to_all | solution.py:1195
  182.3 5.2 %back_e2.1 = (f32[92,64,128]{2,1,0:T(8,128)S(1)}, f32[92,64,128]{2,1,0:T(8,128)S(1)}, f32[32,128]{1,0:T(8,128)S(1)}, f32[96,256]{1,0:T(8,128)S(1)}, f32[96,256]{1,0:T(8,128)S(1)}) custom-call(s32[8,128]{1,0:T(8,128)S(1)} %get-tuple-element.129.refs_0_, s32[1]{0:T(128)} %bitcast.refs_0_.refs_1_, f32[92,64,128]{2,1,0:T(8,128)S(1)} %get-tuple-element.177.refs_11_.refs_2_, ...), custom_call_target="tpu_custom_call" | custom-call | bytes 14000000 | tf_op jit(solution)/shard_map/back_e2/pallas_call | solution.py:39
  187.6 8.8 %all_to_all.198 = f32[32,1,128]{2,1,0:T(1,128)S(1)} all-to-all(f32[32,1,128]{2,1,0:T(1,128)S(1)} %bitcast.106), channel_id=1, replica_groups=mesh['rows'=16,'ch'=2] {'rows','ch'}, dimensions={0} | all-to-all | bytes 32768 | tf_op jit(solution)/shard_map/all_to_all | solution.py:1195
  196.4 4.8 %back_h2.1 = (f32[92,64,128]{2,1,0:T(8,128)S(1)}, f32[32,128]{1,0:T(8,128)S(1)}, f32[96,256]{1,0:T(8,128)S(1)}, f32[96,256]{1,0:T(8,128)S(1)}) custom-call(s32[8,128]{1,0:T(8,128)S(1)} %get-tuple-element.129.refs_0_, s32[1]{0:T(128)} %bitcast.refs_0_.refs_1_, f32[92,64,128]{2,1,0:T(8,128)S(1)} %get-tuple-element.187.refs_2_, ...), custom_call_target="tpu_custom_call" | custom-call | bytes 14000000 | tf_op jit(solution)/shard_map/back_h2/pallas_call | solution.py:39
  201.2 8.8 %all_to_all.199 = f32[32,1,128]{2,1,0:T(1,128)S(1)} all-to-all(f32[32,1,128]{2,1,0:T(1,128)S(1)} %bitcast.110), channel_id=1, replica_groups=mesh['rows'=16,'ch'=2] {'rows','ch'}, dimensions={0} | all-to-all | bytes 32768 | tf_op jit(solution)/shard_map/all_to_all | solution.py:1195
  210.1 5.0 %back_e1.1 = (f32[92,64,128]{2,1,0:T(8,128)S(1)}, f32[68,32,128]{2,1,0:T(8,128)S(1)}, f32[32,128]{1,0:T(8,128)S(1)}, f32[96,256]{1,0:T(8,128)S(1)}, f32[96,256]{1,0:T(8,128)S(1)}) custom-call(s32[8,128]{1,0:T(8,128)S(1)} %get-tuple-element.129.refs_0_, s32[1]{0:T(128)} %bitcast.refs_0_.refs_1_, f32[92,64,128]{2,1,0:T(8,128)S(1)} %get-tuple-element.191.refs_2_, ...), custom_call_target="tpu_custom_call" | custom-call | bytes 14000000 | tf_op jit(solution)/shard_map/back_e1/pallas_call | solution.py:39
  215.1 8.8 %all_to_all.200 = f32[32,1,128]{2,1,0:T(1,128)S(1)} all-to-all(f32[32,1,128]{2,1,0:T(1,128)S(1)} %bitcast.105), channel_id=1, replica_groups=mesh['rows'=16,'ch'=2] {'rows','ch'}, dimensions={0} | all-to-all | bytes 32768 | tf_op jit(solution)/shard_map/all_to_all | solution.py:1195
  223.9 3.6 %back_h0.1 = (f32[68,32,128]{2,1,0:T(8,128)S(1)}, f32[8,128]{1,0:T(8,128)S(1)}, f32[96,128]{1,0:T(8,128)S(1)}, f32[96,128]{1,0:T(8,128)S(1)}) custom-call(s32[8,128]{1,0:T(8,128)S(1)} %get-tuple-element.129.refs_0_, s32[1]{0:T(128)} %bitcast.refs_0_.refs_1_, f32[92,64,128]{2,1,0:T(8,128)S(1)} %get-tuple-element.196.refs_2_, ...), custom_call_target="tpu_custom_call" | custom-call | bytes 14000000 | tf_op jit(solution)/shard_map/back_h0/pallas_call | solution.py:39
  227.5 0.1 pack_grads.1
  227.6 0.1 collective-permute-start.5
  227.7 2.2 decode.1
  230.0 0.4 pack_maps.1
  230.3 0.6 collective-permute-start.4
  230.9 0.8 join_grads.1
  231.7 3.6 %all-to-all-start.15 = ((bf16[16,96,128]{2,1,0:T(8,128)(2,1)}), bf16[16,96,128]{2,1,0:T(8,128)(2,1)S(1)}, u32[]{:S(2)}, u32[]{:S(2)}) async-start(bf16[16,96,128]{2,1,0:T(8,128)(2,1)} %bitcast.49), calls=%async_computation.15 | async-start | bytes 786432 | tf_op jit(solution)/shard_map/all_to_all | solution.py:1379
  235.3 3.4 %flat_skip.1.refs_1_ = f32[32,14336]{1,0:T(8,128)} custom-call(s32[1]{0:T(128)} %bitcast.refs_0_.refs_1_, bf16[68,32,128]{2,1,0:T(8,128)(2,1)} %copy-done.6, bf16[128,32,128]{2,1,0:T(8,128)(2,1)} %collective-permute-done.4.refs_2_), custom_call_target="tpu_custom_call" | custom-call | bytes 700000 | tf_op jit(solution)/shard_map/flat_skip/pallas_call | solution.py:39
  238.7 3.4 %flat_decoded.1.refs_2_ = f32[32,14336]{1,0:T(8,128)} custom-call(s32[1]{0:T(128)} %bitcast.refs_0_.refs_1_, bf16[68,32,128]{2,1,0:T(8,128)(2,1)} %copy-done.7, bf16[128,32,128]{2,1,0:T(8,128)(2,1)} %collective-permute-done.4.refs_2_), custom_call_target="tpu_custom_call" | custom-call | bytes 700000 | tf_op jit(solution)/shard_map/flat_decoded/pallas_call | solution.py:39
  242.2 6.2 %all-to-all-done.15 = bf16[16,96,128]{2,1,0:T(8,128)(2,1)S(1)} async-done(((bf16[16,96,128]{2,1,0:T(8,128)(2,1)}), bf16[16,96,128]{2,1,0:T(8,128)(2,1)S(1)}, u32[]{:S(2)}, u32[]{:S(2)}) %all-to-all-start.15) | async-done | bytes 393248 | tf_op jit(solution)/shard_map/all_to_all | solution.py:1379
  248.4 0.7 copy-done.40
  249.2 1.9 add_grads.1
  251.1 3.8 %all-to-all-start.16 = ((bf16[16,80,128]{2,1,0:T(8,128)(2,1)}), bf16[16,80,128]{2,1,0:T(8,128)(2,1)S(1)}, u32[]{:S(2)}, u32[]{:S(2)}) async-start(bf16[16,80,128]{2,1,0:T(8,128)(2,1)} %bitcast.118), calls=%async_computation.16 | async-start | bytes 655360 | tf_op jit(solution)/shard_map/all_to_all | solution.py:1407
  254.9 1.2 copy-done.5
  256.1 0.7 copy-done.28
  256.8 0.5 back_pooled.1
  257.4 0.1 collective-permute-start.6
  257.4 1.5 collective-permute-done.6.refs_2_
  259.0 4.0 %pixels_out.1 = f32[16,57344]{1,0:T(8,128)} custom-call(s32[1]{0:T(128)} %bitcast.refs_0_.refs_1_, bf16[64,16,128]{2,1,0:T(8,128)(2,1)S(1)} %get-tuple-element.228.refs_1_, bf16[64,16,128]{2,1,0:T(8,128)(2,1)S(1)} %collective-permute-done.6.refs_2_), custom_call_target="tpu_custom_call" | custom-call | bytes 1750000 | tf_op jit(solution)/shard_map/pixels_out/pallas_call | solution.py:39
  263.0 2.6 all-to-all-done.16
  265.7 1.4 finish.1
  (86 shorter events, 0.3 us)
Async XLA Ops:
  0.7 8.2 %copy-start.27 = (bf16[3,256,32]{1,2,0:T(8,128)(2,1)S(1)}, bf16[3,256,32]{1,2,0:T(8,128)(2,1)}, u32[]{:S(2)}) copy-start(bf16[3,256,32]{1,2,0:T(8,128)(2,1)} %param.34) | copy-start | bytes 147460
  0.7 8.2 %copy-start.33 = (f32[5,32]{1,0:T(8,128)S(1)}, f32[5,32]{1,0:T(8,128)}, u32[]{:S(2)}) copy-start(f32[5,32]{1,0:T(8,128)} %refs_11_.1) | copy-start | bytes 1924
  0.7 8.2 %copy-start.32 = (f32[5,32]{1,0:T(8,128)S(1)}, f32[5,32]{1,0:T(8,128)}, u32[]{:S(2)}) copy-start(f32[5,32]{1,0:T(8,128)} %refs_10_.1) | copy-start | bytes 1924
  0.7 8.2 %copy-start.31 = (bf16[64,32]{0,1:T(8,128)(2,1)S(1)}, bf16[64,32]{0,1:T(8,128)(2,1)}, u32[]{:S(2)}) copy-start(bf16[64,32]{0,1:T(8,128)(2,1)} %param.31) | copy-start | bytes 12292
  0.7 8.2 %copy-start.10 = (bf16[4,3,3,64,32]{3,4,2,1,0:T(8,128)(2,1)S(1)}, bf16[4,3,3,64,32]{3,4,2,1,0:T(8,128)(2,1)}, u32[]{:S(2)}) copy-start(bf16[4,3,3,64,32]{3,4,2,1,0:T(8,128)(2,1)} %param.30) | copy-start | bytes 442372
  0.7 8.2 %copy-start.35 = (f32[3,32]{1,0:T(4,128)S(1)}, f32[3,32]{1,0:T(4,128)}, u32[]{:S(2)}) copy-start(f32[3,32]{1,0:T(4,128)} %refs_9_.1) | copy-start | bytes 1156
  0.7 8.2 %copy-start.34 = (f32[3,32]{1,0:T(4,128)S(1)}, f32[3,32]{1,0:T(4,128)}, u32[]{:S(2)}) copy-start(f32[3,32]{1,0:T(4,128)} %refs_8_.1) | copy-start | bytes 1156
  0.7 8.2 %copy-start.37 = (f32[2,16]{1,0:T(2,128)S(1)}, f32[2,16]{1,0:T(2,128)}, u32[]{:S(2)}) copy-start(f32[2,16]{1,0:T(2,128)} %refs_7_.1) | copy-start | bytes 388
  0.7 8.2 %copy-start.36 = (f32[2,16]{1,0:T(2,128)S(1)}, f32[2,16]{1,0:T(2,128)}, u32[]{:S(2)}) copy-start(f32[2,16]{1,0:T(2,128)} %refs_6_.1) | copy-start | bytes 388
  0.7 8.2 %copy-start.30 = (bf16[32,32]{1,0:T(8,128)(2,1)S(1)}, bf16[32,32]{1,0:T(8,128)(2,1)}, u32[]{:S(2)}) copy-start(bf16[32,32]{1,0:T(8,128)(2,1)} %refs_3_.3) | copy-start | bytes 6148
  0.8 8.2 %copy-start.11 = (bf16[3,3,3,64,32]{3,4,2,1,0:T(8,128)(2,1)S(1)}, bf16[3,3,3,64,32]{3,4,2,1,0:T(8,128)(2,1)}, u32[]{:S(2)}) copy-start(bf16[3,3,3,64,32]{3,4,2,1,0:T(8,128)(2,1)} %param.24) | copy-start | bytes 331780
  0.8 8.2 %copy-start.26 = (bf16[3,3,32,32]{3,2,1,0:T(8,128)(2,1)S(1)}, bf16[3,3,32,32]{3,2,1,0:T(8,128)(2,1)}, u32[]{:S(2)}) copy-start(bf16[3,3,32,32]{3,2,1,0:T(8,128)(2,1)} %refs_0_.1) | copy-start | bytes 55300
  0.8 15.1 %copy-start.38 = (s32[18]{0:T(128)S(1)}, s32[18]{0:T(128)}, u32[]{:S(2)}) copy-start(s32[18]{0:T(128)} %refs_1_.2) | copy-start | bytes 220
  0.8 15.1 %copy-start.39 = (s32[18]{0:T(128)S(1)}, s32[18]{0:T(128)}, u32[]{:S(2)}) copy-start(s32[18]{0:T(128)} %refs_2_.2) | copy-start | bytes 220
  0.8 15.7 %copy-start.3 = (bf16[128,28,256]{2,0,1:T(8,128)(2,1)S(1)}, bf16[128,28,256]{2,0,1:T(8,128)(2,1)}, u32[]{:S(2)}) copy-start(bf16[128,28,256]{2,0,1:T(8,128)(2,1)} %param.20) | copy-start | bytes 5505028
  8.3 8.5 %copy-start.29 = (f32[32,128]{1,0:T(8,128)S(1)}, f32[32,128]{1,0:T(8,128)}, u32[]{:S(2)}) copy-start(f32[32,128]{1,0:T(8,128)} %get-tuple-element.134.refs_1_) | copy-start | bytes 49156
  8.3 24.7 %collective-permute-start = (bf16[78,96,128]{2,1,0:T(8,128)(2,1)}, bf16[78,96,128]{2,1,0:T(8,128)(2,1)}, u32[]{:S(2)}, u32[]{:S(2)}) collective-permute-start(bf16[78,96,128]{2,1,0:T(8,128)(2,1)} %get-tuple-element.131), channel_id=1, source_target_pairs={{0,1},{1,0},{2,3},{3,2},{4,5},{5,4},{6,7},{7,6},{8,9},{9,8},{10,11... | collective-permute-start | bytes 5750792 | tf_op jit(solution)/shard_map/ppermute | solution.py:808
  9.6 7.2 %collective-permute-start.3 = (bf16[44,32,128]{2,1,0:T(8,128)(2,1)S(1)}, bf16[44,32,128]{2,1,0:T(8,128)(2,1)S(1)}, u32[]{:S(2)}, u32[]{:S(2)}) collective-permute-start(bf16[44,32,128]{2,1,0:T(8,128)(2,1)S(1)} %get-tuple-element.135.refs_2_.refs_4_), channel_id=1, source_target_pairs={{0,1},{1,0},{2,3},{3,2},{4,5},{5,4},{6,7},{7,6},{8,9},{9,8},{10,11... | collective-permute-start | bytes 1081352 | tf_op jit(solution)/shard_map/ppermute | solution.py:1231
  9.7 16.3 %collective-permute-start.1 = (bf16[31,32,128]{2,1,0:T(8,128)(2,1)}, bf16[31,32,128]{2,1,0:T(8,128)(2,1)S(1)}, u32[]{:S(2)}, u32[]{:S(2)}) collective-permute-start(bf16[31,32,128]{2,1,0:T(8,128)(2,1)} %get-tuple-element.132), channel_id=1, source_target_pairs={{0,2},{3,1},{2,4},{5,3},{4,6},{7,5},{6,8},{9,7},{8,10},{11,9},{10,... | collective-permute-start | bytes 761864 | tf_op jit(solution)/shard_map/ppermute | solution.py:809
  14.5 11.4 %collective-permute-start.2 = (bf16[31,32,128]{2,1,0:T(8,128)(2,1)}, bf16[31,32,128]{2,1,0:T(8,128)(2,1)}, u32[]{:S(2)}, u32[]{:S(2)}) collective-permute-start(bf16[31,32,128]{2,1,0:T(8,128)(2,1)} %get-tuple-element.133), channel_id=1, source_target_pairs={{1,2},{2,1},{3,4},{4,3},{5,6},{6,5},{7,8},{8,7},{9,10},{10,9},{11,... | collective-permute-start | bytes 761864 | tf_op jit(solution)/shard_map/ppermute | solution.py:810
  19.3 13.8 %all-to-all-start = ((f32[32,1,128]{2,1,0:T(1,128)}), f32[32,1,128]{2,1,0:T(1,128)S(1)}, u32[]{:S(2)}, u32[]{:S(2)}) async-start(f32[32,1,128]{2,1,0:T(1,128)} %bitcast.8), calls=%async_computation | async-start | bytes 32768 | tf_op jit(solution)/shard_map/all_to_all | solution.py:1195
  33.0 1.5 copy-start.2
  36.5 187.5 %copy-start = (f32[92,32,128]{2,1,0:T(8,128)}, f32[92,32,128]{2,1,0:T(8,128)S(1)}, u32[]{:S(2)}) copy-start(f32[92,32,128]{2,1,0:T(8,128)S(1)} %get-tuple-element.140.refs_1_.refs_8_.refs_3_) | copy-start | bytes 4521988
  39.4 184.6 %copy-start.24 = (f32[2,32,128]{2,1,0:T(8,128)}, f32[2,32,128]{2,1,0:T(8,128)S(1)}, u32[]{:S(2)}) copy-start(f32[2,32,128]{2,1,0:T(8,128)S(1)} %get-tuple-element.198.refs_9_.refs_4_) | copy-start | bytes 98308
  137.9 5.5 %copy-start.12 = (f32[32,1,128]{2,1,0:T(1,128)}, f32[32,1,128]{2,1,0:T(1,128)S(1)}, u32[]{:S(2)}) copy-start(f32[32,1,128]{2,1,0:T(1,128)S(1)} %all_to_all.194) | copy-start | bytes 49156
  152.3 6.1 %copy-start.22 = (f32[32,1,128]{2,1,0:T(1,128)}, f32[32,1,128]{2,1,0:T(1,128)S(1)}, u32[]{:S(2)}) copy-start(f32[32,1,128]{2,1,0:T(1,128)S(1)} %all_to_all.195) | copy-start | bytes 49156
  167.3 6.0 %copy-start.14 = (f32[32,1,128]{2,1,0:T(1,128)}, f32[32,1,128]{2,1,0:T(1,128)S(1)}, u32[]{:S(2)}) copy-start(f32[32,1,128]{2,1,0:T(1,128)S(1)} %all_to_all.196) | copy-start | bytes 49156
  173.3 14.2 %copy-start.6 = (bf16[68,32,128]{2,1,0:T(8,128)(2,1)}, bf16[68,32,128]{2,1,0:T(8,128)(2,1)S(1)}, u32[]{:S(2)}) copy-start(bf16[68,32,128]{2,1,0:T(8,128)(2,1)S(1)} %get-tuple-element.226.refs_1_) | copy-start | bytes 1671172
  182.3 5.3 %copy-start.8 = (f32[32,2,128]{2,1,0:T(2,128)}, f32[32,2,128]{2,1,0:T(2,128)S(1)}, u32[]{:S(2)}) copy-start(f32[32,2,128]{2,1,0:T(2,128)S(1)} %all_to_all.197) | copy-start | bytes 98308
  196.4 4.8 %copy-start.16 = (f32[32,1,128]{2,1,0:T(1,128)}, f32[32,1,128]{2,1,0:T(1,128)S(1)}, u32[]{:S(2)}) copy-start(f32[32,1,128]{2,1,0:T(1,128)S(1)} %all_to_all.198) | copy-start | bytes 49156
  210.1 5.0 %copy-start.18 = (f32[32,1,128]{2,1,0:T(1,128)}, f32[32,1,128]{2,1,0:T(1,128)S(1)}, u32[]{:S(2)}) copy-start(f32[32,1,128]{2,1,0:T(1,128)S(1)} %all_to_all.199) | copy-start | bytes 49156
  223.9 3.6 %copy-start.20 = (f32[32,1,128]{2,1,0:T(1,128)}, f32[32,1,128]{2,1,0:T(1,128)S(1)}, u32[]{:S(2)}) copy-start(f32[32,1,128]{2,1,0:T(1,128)S(1)} %all_to_all.200) | copy-start | bytes 49156
  227.5 2.4 copy-start.4
  227.6 3.3 %collective-permute-start.5 = (bf16[1264,128]{1,0:T(8,128)(2,1)S(1)}, bf16[1264,128]{1,0:T(8,128)(2,1)S(1)}, u32[]{:S(2)}, u32[]{:S(2)}) collective-permute-start(bf16[1264,128]{1,0:T(8,128)(2,1)S(1)} %pack_grads.1), channel_id=1, source_target_pairs={{0,1},{1,0},{2,3},{3,2},{4,5},{5,4},{6,7},{7,6},{8,9},{9,8},{10,11... | collective-permute-start | bytes 970760 | tf_op jit(solution)/shard_map/ppermute | solution.py:1373
  229.9 1.0 copy-start.7
  230.3 5.0 %collective-permute-start.4 = (bf16[128,32,128]{2,1,0:T(8,128)(2,1)S(1)}, bf16[128,32,128]{2,1,0:T(8,128)(2,1)}, u32[]{:S(2)}, u32[]{:S(2)}) collective-permute-start(bf16[128,32,128]{2,1,0:T(8,128)(2,1)S(1)} %pack_maps.1), channel_id=1, source_target_pairs={{0,1},{1,0},{2,3},{3,2},{4,5},{5,4},{6,7},{7,6},{8,9},{9,8},{10,11... | collective-permute-start | bytes 3145736 | tf_op jit(solution)/shard_map/ppermute | solution.py:1391
  231.7 16.7 %all-to-all-start.15 = ((bf16[16,96,128]{2,1,0:T(8,128)(2,1)}), bf16[16,96,128]{2,1,0:T(8,128)(2,1)S(1)}, u32[]{:S(2)}, u32[]{:S(2)}) async-start(bf16[16,96,128]{2,1,0:T(8,128)(2,1)} %bitcast.49), calls=%async_computation.15 | async-start | bytes 786432 | tf_op jit(solution)/shard_map/all_to_all | solution.py:1379
  248.4 0.7 copy-start.40
  249.2 5.7 %copy-start.1 = (f32[92,32,128]{2,1,0:T(8,128)S(1)}, f32[92,32,128]{2,1,0:T(8,128)}, u32[]{:S(2)}) copy-start(f32[92,32,128]{2,1,0:T(8,128)} %copy-done) | copy-start | bytes 4521988
  249.2 5.7 %copy-start.25 = (f32[2,32,128]{2,1,0:T(8,128)S(1)}, f32[2,32,128]{2,1,0:T(8,128)}, u32[]{:S(2)}) copy-start(f32[2,32,128]{2,1,0:T(8,128)} %copy-done.24) | copy-start | bytes 98308
  251.1 14.6 %all-to-all-start.16 = ((bf16[16,80,128]{2,1,0:T(8,128)(2,1)}), bf16[16,80,128]{2,1,0:T(8,128)(2,1)S(1)}, u32[]{:S(2)}, u32[]{:S(2)}) async-start(bf16[16,80,128]{2,1,0:T(8,128)(2,1)} %bitcast.118), calls=%async_computation.16 | async-start | bytes 655360 | tf_op jit(solution)/shard_map/all_to_all | solution.py:1407
  254.9 1.2 copy-start.5
  256.1 0.7 copy-start.28
  257.4 1.6 collective-permute-start.6
  259.0 6.7 %copy-start.9 = (f32[32,2,128]{2,1,0:T(2,128)S(1)}, f32[32,2,128]{2,1,0:T(2,128)}, u32[]{:S(2)}) copy-start(f32[32,2,128]{2,1,0:T(2,128)} %copy-done.8) | copy-start | bytes 98308
  259.0 6.7 %copy-start.13 = (f32[32,1,128]{2,1,0:T(1,128)S(1)}, f32[32,1,128]{2,1,0:T(1,128)}, u32[]{:S(2)}) copy-start(f32[32,1,128]{2,1,0:T(1,128)} %copy-done.12) | copy-start | bytes 49156
  259.0 6.7 %copy-start.15 = (f32[32,1,128]{2,1,0:T(1,128)S(1)}, f32[32,1,128]{2,1,0:T(1,128)}, u32[]{:S(2)}) copy-start(f32[32,1,128]{2,1,0:T(1,128)} %copy-done.14) | copy-start | bytes 49156
  259.0 6.7 %copy-start.17 = (f32[32,1,128]{2,1,0:T(1,128)S(1)}, f32[32,1,128]{2,1,0:T(1,128)}, u32[]{:S(2)}) copy-start(f32[32,1,128]{2,1,0:T(1,128)} %copy-done.16) | copy-start | bytes 49156
  259.0 6.7 %copy-start.19 = (f32[32,1,128]{2,1,0:T(1,128)S(1)}, f32[32,1,128]{2,1,0:T(1,128)}, u32[]{:S(2)}) copy-start(f32[32,1,128]{2,1,0:T(1,128)} %copy-done.18) | copy-start | bytes 49156
  259.0 6.7 %copy-start.21 = (f32[32,1,128]{2,1,0:T(1,128)S(1)}, f32[32,1,128]{2,1,0:T(1,128)}, u32[]{:S(2)}) copy-start(f32[32,1,128]{2,1,0:T(1,128)} %copy-done.20) | copy-start | bytes 49156
  259.0 6.7 %copy-start.23 = (f32[32,1,128]{2,1,0:T(1,128)S(1)}, f32[32,1,128]{2,1,0:T(1,128)}, u32[]{:S(2)}) copy-start(f32[32,1,128]{2,1,0:T(1,128)} %copy-done.22) | copy-start | bytes 49156
